TPU v7x, 128 devices: a whole 4x4x4 slice. The times are simulated.
128 devices in a mesh: dp: 8 (over y, core), fsdp: 16 (over x, z).
Axes of the slice: x: 4, y: 4, z: 4, core: 2. Of those that a mesh axis runs over, the one named last changes fastest.
Arguments:
- hidden: bfloat16 [8192, 14784], P('fsdp', 'dp'), may hold values from -6 to 6
- cotangent: bfloat16 [8192, 8192], P('fsdp', 'dp'), may hold values from -6 to 6
- down_weight: bfloat16 [14784, 8192], P('dp', 'fsdp'), may hold values from -0.046875 to 0.046875
- adapter_in: bfloat16 [16, 64, 14784], P(None, None, 'dp'), may hold values from -0.046875 to 0.046875
- adapter_out: bfloat16 [16, 64, 8192], P(None, None, 'dp'), may hold values from -0.0625 to 0.0625
- adapter_ids: int32 [64, 1], P('fsdp'), may hold values from 0 to 15
- adapter_slot: int32 [16], replicated, may hold values from 0 to 15, each once
Outputs:
- hidden_gradient: bfloat16 [8192, 14784], P('fsdp', 'dp')
- grad_in: bfloat16 [16, 64, 14784], P('fsdp', None, 'dp')
- grad_out: bfloat16 [16, 64, 8192], P('fsdp', None, 'dp')
Inputs may be any that keep to these rules, and one draw needn't show every extreme that they name: `adapter_ids`: every adapter is named by at least one block. A permutation; adapter a's weights and gradients stand at slot adapter_slot[a].
All inputs are finite; a program needn't handle non-finite values.
Results may differ from a plain program's by a relative error of at most 0.025.
Values may be sent and summed in bfloat16 or wider, within the bound.
No kernel may reach another device: no remote copies, remote signals or barrier semaphores. Data moves between devices by JAX's collectives and lax.ppermute only.
A program may use at most 192 MiB of HBM per device.

v0:
```python
import math

import jax
import jax.numpy as jnp
from jax import lax
from jax.sharding import PartitionSpec as P

adapter_scale = 2.0


def body(hidden, cotangent, down_weight, adapter_in, adapter_out, adapter_ids, adapter_slot):
    count_of_rows = hidden.shape[0]
    block_count = adapter_ids.shape[0]
    block_rows = count_of_rows // block_count
    slot_index = adapter_slot[adapter_ids[:, 0]]
    chosen_in = jnp.take(adapter_in, slot_index, axis=0)
    chosen_out = jnp.take(adapter_out, slot_index, axis=0)
    hidden_blocks = hidden.reshape(block_count, block_rows, hidden.shape[1])
    cotangent_blocks = cotangent.reshape(block_count, block_rows, cotangent.shape[1])
    partial_project = jnp.einsum(
        "btd,brd->btr", cotangent_blocks, chosen_out, preferred_element_type=jnp.float32
    )
    partial_reduced = jnp.einsum(
        "btf,brf->btr", hidden_blocks, chosen_in, preferred_element_type=jnp.float32
    )
    rank_width = chosen_in.shape[1]
    summed = lax.psum(
        jnp.concatenate([partial_project, partial_reduced], axis=2).astype(jnp.bfloat16), "dp"
    ).astype(jnp.float32)
    project = summed[:, :, :rank_width].astype(jnp.bfloat16)
    reduced = summed[:, :, rank_width:].astype(jnp.bfloat16)
    gathered = lax.all_gather(cotangent, "dp", axis=1, tiled=True)
    frozen_path_gradient = lax.dot_general(
        gathered,
        lax.all_gather(down_weight, "fsdp", axis=1, tiled=True),
        (((1,), (1,)), ((), ())),
        preferred_element_type=jnp.float32,
    )
    reduced_rank_product = jnp.einsum(
        "btr,brf->btf", project, chosen_in, preferred_element_type=jnp.float32
    )
    reduced_rank_product = reduced_rank_product.reshape(count_of_rows, hidden.shape[1])
    hidden_gradient = (frozen_path_gradient + adapter_scale * reduced_rank_product).astype(
        jnp.bfloat16
    )
    adapter_multiplier = adapter_scale / math.sqrt(count_of_rows)
    block_in = (
        jnp.einsum("btr,btf->brf", project, hidden_blocks, preferred_element_type=jnp.float32)
        * adapter_multiplier
    )
    block_out = (
        jnp.einsum("btr,btd->brd", reduced, cotangent_blocks, preferred_element_type=jnp.float32)
        * adapter_multiplier
    )
    onehot = (
        slot_index[:, None] == jnp.arange(adapter_in.shape[0], dtype=jnp.int32)[None, :]
    ).astype(jnp.float32)
    device_in = jnp.einsum("ba,brf->arf", onehot, block_in, precision=lax.Precision.HIGHEST)
    device_out = jnp.einsum("ba,brd->ard", onehot, block_out, precision=lax.Precision.HIGHEST)
    grad_in, grad_out = (
        lax.psum_scatter(
            device_in.astype(jnp.bfloat16), "fsdp", scatter_dimension=0, tiled=True
        ).astype(jnp.float32),
        lax.psum_scatter(
            device_out.astype(jnp.bfloat16), "fsdp", scatter_dimension=0, tiled=True
        ).astype(jnp.float32),
    )
    return (hidden_gradient, grad_in.astype(jnp.bfloat16), grad_out.astype(jnp.bfloat16))


def solution(mesh):
    placed = (
        P("fsdp", "dp"),
        P("fsdp", "dp"),
        P("dp", "fsdp"),
        P(None, None, "dp"),
        P(None, None, "dp"),
        P("fsdp", None),
        P(),
    )
    return jax.shard_map(
        body,
        mesh=mesh,
        in_specs=placed,
        out_specs=(P("fsdp", "dp"), P("fsdp", None, "dp"), P("fsdp", None, "dp")),
        check_vma=False,
    )
```

profile of v0, /device:TPU:0, one launch (start us, length us, event | category | flops | bytes accessed | tf_op | source)
XLA Modules:
  0.0 486.2 jit_solution(14419794683288921706)
XLA Ops:
  7.2 0.8 fusion.26
  8.0 1.3 gather_fusion
  9.4 2.8 gather_fusion.2
  12.2 1.4 gather_fusion.1
  13.6 2.1 fusion.11
  15.7 0.5 fusion.10
  16.3 0.7 pad_maximum_fusion
  17.0 0.7 all-gather.3.cloned.1.call-update
  17.8 0.7 all-gather.5.cloned.1.call-update
  18.5 60.3 %all-reduce.4.cloned.1.call-done = bf16[4,128,128]{1,2,0:T(8,128)(2,1)} async-done(((bf16[4,128,128]{1,2,0:T(8,128)(2,1)}), bf16[4,128,128]{1,2,0:T(8,128)(2,1)}) %all-reduce.4.cloned.1.call-update) | async-done | bytes 131088 | tf_op jit(solution)/shard_map/psum | solution.py:27
  78.8 1.1 convolution_multiply_fusion.1
  79.9 2.5 convolution_convert_fusion.1
  82.5 2.5 copy.24
  85.0 0.2 reduce-scatter.7.cloned.1.call-start
  85.2 0.6 copy-done.5
  85.9 2.2 convolution_multiply_fusion
  88.1 4.5 convolution_convert_fusion
  92.7 2.8 copy.22
  95.5 3.1 multiply_bitcast_fusion
  98.6 30.8 %all-gather.3.cloned.1.call-done = bf16[512,8192]{1,0:T(8,128)(2,1)} async-done(((bf16[512,1024]{1,0:T(8,128)(2,1)}), bf16[512,8192]{1,0:T(8,128)(2,1)}) %all-gather.3.cloned.1.call-update) | async-done | bytes 8388624 | tf_op jit(solution)/shard_map/all_gather | solution.py:32
  129.3 192.5 %all-gather.5.cloned.1.call-done = bf16[1848,8192]{1,0:T(8,128)(2,1)} async-done(((bf16[1848,512]{1,0:T(8,128)(2,1)}), bf16[1848,8192]{1,0:T(8,128)(2,1)}) %all-gather.5.cloned.1.call-update) | async-done | bytes 30277648 | tf_op jit(solution)/shard_map/all_gather | solution.py:35
  321.9 23.3 %fusion = bf16[512,1848]{0,1:T(8,128)(2,1)} fusion(f32[4,231,8,128]{3,2,1,0:T(8,128)} %multiply_bitcast_fusion, bf16[512,8192]{1,0:T(8,128)(2,1)} %all-gather.3.cloned.1.call-done, bf16[1848,8192]{1,0:T(8,128)(2,1)} %all-gather.5.cloned.1.call-done), kind=kOutput, calls=%fused_computation.4 | convolution fusion | flops 15504039936 | bytes 44343296 | tf_op jit(solution)/shard_map/dot_general | solution.py:33
  345.1 54.5 %reduce-scatter.9.cloned.1.call-done = bf16[1,64,1024]{2,1,0:T(8,128)(2,1)} async-done(((bf16[16,64,1024]{2,1,0:T(8,128)(2,1)}), bf16[1,64,1024]{2,1,0:T(8,128)(2,1)}) %reduce-scatter.9.cloned.1.call-update) | async-done | bytes 131088
  399.6 80.0 %reduce-scatter.7.cloned.1.call-done = bf16[1,64,1848]{2,1,0:T(8,128)(2,1)} async-done(((bf16[16,64,1848]{2,1,0:T(8,128)(2,1)}), bf16[1,64,1848]{2,1,0:T(8,128)(2,1)}) %reduce-scatter.7.cloned.1.call-update) | async-done | bytes 236560
  (22 shorter events, 0.3 us)
Async XLA Ops:
  7.2 5.0 %copy-start = (bf16[16,64,1024]{2,1,0:T(8,128)(2,1)S(1)}, bf16[16,64,1024]{2,1,0:T(8,128)(2,1)}, u32[]{:S(2)}) copy-start(bf16[16,64,1024]{2,1,0:T(8,128)(2,1)} %param.11) | copy-start | bytes 6291460
  7.2 71.6 %all-reduce.4.cloned.1.call-start = ((), (), s32[]{:S(2)}) async-start(), calls=%async_computation.4 | async-start | bytes 262144 | tf_op jit(solution)/shard_map/psum | solution.py:27
  13.5 2.2 copy-start.2
  13.6 2.2 copy-start.4
  16.3 62.5 %copy-start.3 = (bf16[512,1024]{1,0:T(8,128)(2,1)S(1)}, bf16[512,1024]{1,0:T(8,128)(2,1)}, u32[]{:S(2)}) copy-start(bf16[512,1024]{1,0:T(8,128)(2,1)} %param.8) | copy-start | bytes 3145732
  17.0 112.4 %all-gather.3.cloned.1.call-start = ((), (), s32[]{:S(2)}) async-start(), calls=%async_computation.2 | async-start | bytes 9437184 | tf_op jit(solution)/shard_map/all_gather | solution.py:32
  17.7 304.1 %all-gather.5.cloned.1.call-start = ((), (), s32[]{:S(2)}) async-start(), calls=%async_computation.3 | async-start | bytes 32169984 | tf_op jit(solution)/shard_map/all_gather | solution.py:35
  18.4 381.2 %reduce-scatter.9.cloned.1.call-start = ((), (), s32[]{:S(2)}) async-start(), calls=%async_computation.6 | async-start | bytes 2228224
  85.0 0.9 copy-start.5
  85.0 394.6 %reduce-scatter.7.cloned.1.call-start = ((), (), s32[]{:S(2)}) async-start(), calls=%async_computation.5 | async-start | bytes 4177920
  321.9 157.8 %copy-start.1 = (bf16[16,64,1024]{2,1,0:T(8,128)(2,1)S(1)}, bf16[16,64,1024]{2,1,0:T(8,128)(2,1)}, u32[]{:S(2)}) copy-start(bf16[16,64,1024]{2,1,0:T(8,128)(2,1)} %param.11) | copy-start | bytes 6291460
Sparse Core Ops, SparseCore 0:
  17.1 61.6 all-reduce.3
  80.6 48.7 all-gather.2
  131.7 190.1 all-gather.4
  325.9 73.7 reduce-scatter.8
  403.5 76.1 reduce-scatter.6
where the time goes:
time: 486 us
  waiting for transfers between devices  420 us (86%)
  matrix products  39.5 us (8%)
  between operations  13.9 us (3%)
  local copies, waits for them, and re-layouts  11.4 us (2%)
    all_gather x1, waiting for transfers between devices, body(): lax.all_gather(down_weight, 'fsdp', axis=1, tiled=True)  193 us
    unnamed x7, waiting for transfers between devices  136 us
    psum x1, waiting for transfers between devices, body(): lax.psum(jnp.concatenate([partial_project, partial_reduced], axis=2).asty...  60.3 us
    all_gather x1, waiting for transfers between devices, body(): gathered = lax.all_gather(cotangent, 'dp', axis=1, tiled=True)  30.8 us
    dot_general x1, matrix products, body(): lax.dot_general(gathered, lax.all_gather(down_weight, 'fsdp', axis=1, til...  23.3 us
  transfers between devices with their start and end apart: 5, of which 5 were waited for; matrix products, arithmetic and copies ran while one was open for 9% of the time, Pallas kernels for 0%

commit v1 on v0

v1 whole, which is shorter than its diff:
```python
import math

import jax
import jax.numpy as jnp
from jax import lax
from jax.experimental import pallas as pl
from jax.experimental.pallas import tpu as pltpu
from jax.sharding import Mesh, PartitionSpec as P

adapter_scale = 2.0
N = 4
MIB = 1024 * 1024
NN = (((1,), (0,)), ((), ()))
NT = (((1,), (1,)), ((), ()))
TN = (((0,), (0,)), ((), ()))


def take_from(array, axis, step):
    return lax.ppermute(array, axis, [((i + step) % N, i) for i in range(N)])


def other_core(array):
    return lax.ppermute(array, "c", [(0, 1), (1, 0)])


def sum_over_dp(array):
    array = array + other_core(array)
    array = array + lax.ppermute(array, "y", [(0, 1), (1, 0), (2, 3), (3, 2)])
    return array + lax.ppermute(array, "y", [(0, 3), (3, 0), (1, 2), (2, 1)])


def scatter_ring(far, right, left, own, axis, way):
    via = take_from(far, axis, -way)
    if way > 0:
        left = take_from(left, axis, 1)
        right = take_from(right + via, axis, -1)
    else:
        right = take_from(right, axis, -1)
        left = take_from(left + via, axis, 1)
    return [own, left, right]


def whole(array):
    return pl.BlockSpec(array.shape, lambda i, ix: (0,) * array.ndim)


def call(kernel, grid, operands, in_specs, out_specs, out_shape, scratch, mib):
    return pl.pallas_call(
        kernel,
        grid_spec=pltpu.PrefetchScalarGridSpec(
            num_scalar_prefetch=1,
            grid=grid,
            in_specs=in_specs,
            out_specs=out_specs,
            scratch_shapes=scratch,
        ),
        out_shape=out_shape,
        compiler_params=pltpu.CompilerParams(vmem_limit_bytes=mib * MIB),
        cost_estimate=pl.CostEstimate(flops=1000000, bytes_accessed=1000000, transcendentals=0),
    )(*operands)


def rank_sums(slots, cotangent, hidden, adapter_out, adapter_in):
    tokens, width = cotangent.shape
    units = hidden.shape[0]
    rank = adapter_in.shape[1]
    blocks = slots.shape[0]
    rows = tokens // blocks

    def kernel(slots, cotangent, hidden, a_out, a_in, out, cot, hid, outs, ins, sems):
        copies = [
            pltpu.make_async_copy(cotangent, cot, sems.at[0]),
            pltpu.make_async_copy(hidden, hid, sems.at[1]),
        ]
        for b in range(blocks):
            copies.append(pltpu.make_async_copy(a_out.at[slots[b]], outs.at[b], sems.at[2 + b]))
        for b in range(blocks):
            copies.append(
                pltpu.make_async_copy(a_in.at[slots[b]], ins.at[b], sems.at[2 + blocks + b])
            )
        for copy in copies:
            copy.start()
        for copy in copies:
            copy.wait()
        for b in range(blocks):
            at = slice(b * rows, (b + 1) * rows)
            out[:rank, at] = lax.dot_general(
                outs[b], cot[at, :], NT, preferred_element_type=jnp.float32
            ).astype(out.dtype)
            out[rank:, at] = lax.dot_general(
                ins[b], hid[:, at], NN, preferred_element_type=jnp.float32
            ).astype(out.dtype)

    far = pl.BlockSpec(memory_space=pltpu.HBM)
    return call(
        kernel,
        (1,),
        (slots, cotangent, hidden, adapter_out, adapter_in),
        [far] * 4,
        pl.BlockSpec(memory_space=pltpu.VMEM),
        jax.ShapeDtypeStruct((2 * rank, tokens), jnp.bfloat16),
        [
            pltpu.VMEM((tokens, width), jnp.bfloat16),
            pltpu.VMEM((units, tokens), jnp.bfloat16),
            pltpu.VMEM((blocks, rank, width), jnp.bfloat16),
            pltpu.VMEM((blocks, rank, units), jnp.bfloat16),
            pltpu.SemaphoreType.DMA((2 + 2 * blocks,)),
        ],
        8,
    )


def terms_kernel(multiplier, index, summed, cotangent, hidden, *refs):
    outs, products = refs[:8], refs[8]
    blocks = products.shape[0]
    rows = cotangent.shape[0] // blocks
    width = cotangent.shape[1]
    units = hidden.shape[0]
    rank = summed.shape[0] // 2
    for b in range(blocks):
        at = slice(b * rows, (b + 1) * rows)
        products[b, :, :width] = lax.dot_general(
            summed[rank:, at], cotangent[at, :], NN, preferred_element_type=jnp.float32
        )
        products[b, :, width : width + units] = lax.dot_general(
            summed[:rank, at], hidden[:, at], NT, preferred_element_type=jnp.float32
        )
        products[b, :, width + units :] = jnp.zeros(
            (rank, products.shape[2] - width - units), jnp.float32
        )
    x, z = index[blocks], index[blocks + 1]
    for place, s in enumerate((2, 1, 3, 0)):
        for part, t in enumerate((2, 1, 3, 0)):
            slot = lax.rem(x + t, N) * N + lax.rem(z + s, N)
            total = jnp.zeros(products.shape[1:], jnp.float32)
            for b in range(blocks):
                weight = jnp.where(index[b] == slot, jnp.float32(multiplier), jnp.float32(0))
                total = total + weight * products[b]
            ref = outs[place * 2 + part // 2]
            row = part % 2 * rank
            ref[row : row + rank, :] = total.astype(ref.dtype)


def gradient_terms(index, summed, cotangent, hidden, multiplier):
    blocks = index.shape[0] - 2
    wide = cotangent.shape[1] + hidden.shape[0]
    wide = wide + -wide % 128
    rank = summed.shape[0] // 2
    shape = (2 * rank, wide)

    def kernel(*refs):
        terms_kernel(multiplier, *refs)

    return call(
        kernel,
        (1,),
        (index, summed, cotangent, hidden),
        [whole(a) for a in (summed, cotangent, hidden)],
        [pl.BlockSpec(memory_space=pltpu.VMEM)] * 8,
        [jax.ShapeDtypeStruct(shape, jnp.bfloat16)] * 8,
        [pltpu.VMEM((blocks, rank, wide), jnp.float32)],
        20,
    )


def added(refs, at):
    total = refs[0][at, :].astype(jnp.float32)
    for ref in refs[1:]:
        total = total + ref[at, :].astype(jnp.float32)
    return total


def middle_kernel(*refs):
    outs = refs[6:]
    rank = outs[0].shape[0]
    for n, out in enumerate(outs):
        at = slice(n % 2 * rank, (n % 2 + 1) * rank)
        out[...] = added(refs[n // 2 * 3 : n // 2 * 3 + 3], at).astype(out.dtype)


def middle_sums(lows, highs):
    rows, wide = lows[0].shape
    shape = (rows // 2, wide)
    kinds = [jnp.bfloat16] * 3 + [jnp.float32]
    return pl.pallas_call(
        middle_kernel,
        out_shape=[jax.ShapeDtypeStruct(shape, kind) for kind in kinds],
        compiler_params=pltpu.CompilerParams(vmem_limit_bytes=10 * MIB),
        cost_estimate=pl.CostEstimate(flops=1000000, bytes_accessed=1000000, transcendentals=0),
    )(*lows, *highs)


def last_kernel(own, across, before, after, out_in, out_out):
    split, units = out_out.shape[2], out_in.shape[2]
    total = added((own, across, before, after), slice(None))
    out_out[0] = total[:, :split].astype(out_out.dtype)
    out_in[0] = total[:, split : split + units].astype(out_in.dtype)


def last_sum(parts, units, width):
    rank = parts[0].shape[0]
    return pl.pallas_call(
        last_kernel,
        out_shape=[jax.ShapeDtypeStruct((1, rank, n), jnp.bfloat16) for n in (units, width)],
        compiler_params=pltpu.CompilerParams(vmem_limit_bytes=6 * MIB),
        cost_estimate=pl.CostEstimate(flops=1000000, bytes_accessed=1000000, transcendentals=0),
    )(*parts)


def products(index, gathered, weights, steps):
    rows, width = weights[0].shape
    tokens = gathered.shape[3]

    def kernel(index, gathered, *refs):
        pieces, outs, held, sides, sems = refs[:N], refs[N : N + 2], refs[-3], refs[-2], refs[-1]
        copies = {}
        for n, step in enumerate(steps):
            for r in range(N):
                copies[n, r] = pltpu.make_async_copy(
                    gathered.at[lax.rem(index[2] + r, N), index[n], step % 2],
                    sides.at[n, r],
                    sems.at[n, r],
                )
                copies[n, r].start()
                if n == 0:
                    copies[2, r] = pltpu.make_async_copy(pieces[r], held.at[r], sems.at[2, r])
                    copies[2, r].start()
        for n in range(2):
            total = None
            for r in range(N):
                if n == 0:
                    copies[2, r].wait()
                copies[n, r].wait()
                part = lax.dot_general(
                    held[r], sides[n, r], NT, preferred_element_type=jnp.float32
                )
                total = part if total is None else total + part
            outs[n][...] = total.astype(jnp.bfloat16)

    shape = (rows, tokens)
    return call(
        kernel,
        (1,),
        [index, gathered, *weights],
        [pl.BlockSpec(memory_space=pltpu.HBM)] + [pl.BlockSpec(memory_space=pl.ANY)] * N,
        [pl.BlockSpec(memory_space=pltpu.VMEM)] * 2,
        [jax.ShapeDtypeStruct(shape, jnp.bfloat16)] * 2,
        [
            pltpu.VMEM((N, rows, width), jnp.bfloat16),
            pltpu.VMEM((2, N, tokens, width), jnp.bfloat16),
            pltpu.SemaphoreType.DMA((3, N)),
        ],
        20,
    )


def finish_kernel(slots, summed, a_in, *refs):
    out = refs[-1]
    rank = a_in.shape[1]
    low = adapter_scale * lax.dot_general(
        a_in[0], summed[:rank, :], TN, preferred_element_type=jnp.float32
    )
    start = 0
    for k in range(0, len(refs) - 1, 3):
        rows = refs[k].shape[0]
        total = low[start : start + rows] + added(refs[k : k + 3], slice(None))
        out[start : start + rows, :] = total.astype(out.dtype)
        start += rows


def finish(slots, summed, adapter_in, parts):
    twice, tokens = summed.shape
    blocks = slots.shape[0]
    rows = tokens // blocks
    rank, units = adapter_in.shape[1:]
    return call(
        finish_kernel,
        (blocks,),
        [slots, summed, adapter_in] + parts,
        [
            pl.BlockSpec((twice, rows), lambda i, s: (0, i)),
            pl.BlockSpec((1, rank, units), lambda i, s: (s[i], 0, 0)),
        ]
        + [pl.BlockSpec((p.shape[0], rows), lambda i, s: (0, i)) for p in parts],
        pl.BlockSpec((units, rows), lambda i, s: (0, i)),
        jax.ShapeDtypeStruct((units, tokens), jnp.bfloat16),
        [],
        10,
    )


def body(hidden, cotangent, down_weight, adapter_in, adapter_out, adapter_ids, adapter_slot):
    hidden = hidden.T
    units, tokens = hidden.shape
    x = lax.axis_index("x")
    z = lax.axis_index("z")
    slots = adapter_slot[adapter_ids[:, 0]]

    width = cotangent.shape[1] // 2
    turned = []
    for k in range(2):
        at = lax.rem(z + k, 2) * width
        piece = lax.dynamic_slice_in_dim(cotangent, at, width, axis=1)
        pairs = [
            (c * N + d, (d // 2) * N + 2 * c + (d + k) % 2) for c in range(2) for d in range(N)
        ]
        turned.append(lax.ppermute(piece, ("c", "z"), pairs))
    first = (units // 2 + 15) // 16 * 16
    own = [down_weight[:first], down_weight[first:]]
    after = [take_from(p, "x", 1) for p in own]
    before = [take_from(p, "x", -1) for p in own]

    ranks = rank_sums(slots, cotangent, hidden, adapter_out, adapter_in)
    turned[0], turned[1], after[0], before[0], ranks = lax.optimization_barrier(
        (turned[0], turned[1], after[0], before[0], ranks)
    )
    gathered = lax.all_gather(jnp.stack(turned), ("y", "c"))
    gathered = gathered.reshape(N, 2, 2, tokens, width)
    summed = sum_over_dp(ranks)
    index = jnp.concatenate([slots, jnp.stack([x, z]).astype(jnp.int32)])
    terms = gradient_terms(index, summed, cotangent, hidden, adapter_scale / math.sqrt(tokens))
    after[0], after[1], before[1], *terms = lax.optimization_barrier(
        (after[0], after[1], before[1], *terms)
    )
    fars = [take_from(after[0], "x", 1), take_from(before[1], "x", -1)]

    def make(chunk, *steps):
        index = jnp.stack([lax.rem(z + s, N) // 2 for s in steps] + [x]).astype(jnp.int32)
        weights = (own[chunk], after[chunk], fars[chunk], before[chunk])
        return products(index, gathered, weights, steps)

    far0, left0 = make(0, 2, 3)
    far1, right1 = make(1, 2, 1)
    right0, own0 = make(0, 1, 0)
    left1, own1 = make(1, 3, 0)
    parts = scatter_ring(far0, right0, left0, own0, "z", 1)
    parts += scatter_ring(far1, right1, left1, own1, "z", -1)
    hidden_gradient = finish(slots, summed, adapter_in, parts)

    lows = scatter_ring(*terms[0::2], "z", 1)
    highs = scatter_ring(*terms[1::2], "z", -1)
    across, before, after, own = middle_sums(lows, highs)
    others = [take_from(p, "x", s) for p, s in ((across, 2), (before, -1), (after, 1))]
    grad_in, grad_out = last_sum([own] + others, units, cotangent.shape[1])
    return hidden_gradient.T, grad_in, grad_out


def solution(mesh):
    fine = Mesh(mesh.devices.reshape(N, 2, N, N), ("y", "c", "x", "z"))
    dp, fsdp = ("y", "c"), ("x", "z")
    placed = (
        P(fsdp, dp),
        P(fsdp, dp),
        P(dp, fsdp),
        P(None, None, dp),
        P(None, None, dp),
        P(fsdp, None),
        P(),
    )
    return jax.shard_map(
        body,
        mesh=fine,
        in_specs=placed,
        out_specs=(P(fsdp, dp), P(fsdp, None, dp), P(fsdp, None, dp)),
        check_vma=False,
    )
```

time: 486 us -> 199 us (0.41)
  waiting for transfers between devices: 420 us -> 71.6 us
  Pallas kernels: 0 us -> 45.2 us
  matrix products: 39.5 us -> 0 us
  starting transfers between devices: 0.38 us -> 39.3 us
  local copies, waits for them, and re-layouts: 11.4 us -> 19 us
  other arithmetic: 1.49 us -> 8.1 us
    all_gather x2 -> x1, waiting for transfers between devices: 223 us -> 0.01 us  [body(): gathered = lax.all_gather(jnp.stack(turned), ('y', 'c'))]
    unnamed x7 -> x1, waiting for transfers between devices: 136 us -> 0.02 us
    ppermute x0 -> x26, waiting for transfers between devices: none -> 71.5 us  [the longest x21 57.5 us: take_from(): return lax.ppermute(array, axis, [((i + step) % N, i) for i in range(N)])]
    psum x1 -> x0, waiting for transfers between devices: 60.3 us -> none  [body(): lax.psum(jnp.concatenate([partial_project, partial_reduced], axis=2).asty...]
    pallas_call x0 -> x9, Pallas kernels: none -> 45.2 us  [the longest x7 42 us: call(): pl.pallas_call(kernel, grid_spec=pltpu.PrefetchScalarGridSpec(num_scalar_...]
    dot_general x8 -> x0, matrix products: 39.5 us -> none  [the longest x1 23.3 us: body(): lax.dot_general(gathered, lax.all_gather(down_weight, 'fsdp', axis=1, til...]
    ppermute x0 -> x26, starting transfers between devices: none -> 39.2 us  [the longest x21 27.2 us: take_from(): return lax.ppermute(array, axis, [((i + step) % N, i) for i in range(N)])]
    unnamed x12 -> x42, local copies, waits for them, and re-layouts: 0.68 us -> 14.7 us
  transfers between devices with their start and end apart: 5 -> 27, of which waited for: 5 -> 12; matrix products, arithmetic and copies ran while one was open for 9% -> 4% of each run, Pallas kernels for 0% -> 21%
where the time goes in v1:
time: 199 us; the launch traced here: 197 us
  waiting for transfers between devices  71.6 us (36%)
  Pallas kernels  45.2 us (23%)
  starting transfers between devices  39.3 us (20%)
  local copies, waits for them, and re-layouts  19 us (10%)
  between operations  14.3 us (7%)
  other arithmetic  8.1 us (4%)
    ppermute x21, waiting for transfers between devices, take_from(): return lax.ppermute(array, axis, [((i + step) % N, i) for i in range(N)])  57.5 us
    pallas_call x7, Pallas kernels, call(): pl.pallas_call(kernel, grid_spec=pltpu.PrefetchScalarGridSpec(num_scalar_...  42 us
    ppermute x21, starting transfers between devices, take_from(): return lax.ppermute(array, axis, [((i + step) % N, i) for i in range(N)])  27.2 us
    unnamed x42, local copies, waits for them, and re-layouts  14.7 us
    ppermute x2, starting transfers between devices, body(): turned.append(lax.ppermute(piece, ('c', 'z'), pairs))  7.28 us
    ppermute x1, waiting for transfers between devices, sum_over_dp(): return array + lax.ppermute(array, 'y', [(0, 3), (3, 0), (1, 2), (2, 1)])  6.19 us
  transfers between devices with their start and end apart: 27, of which 12 were waited for; matrix products, arithmetic and copies ran while one was open for 4% of the time, Pallas kernels for 21%

profile of v1, /device:TPU:0, one launch (start us, length us, event | category | flops | bytes accessed | tf_op | source)
XLA Modules:
  0.0 197.4 jit_solution(8184661580135513524)
XLA Ops:
  8.6 2.9 %collective-permute-start.2 = (bf16[928,512]{1,0:T(8,128)(2,1)S(1)}, bf16[928,512]{1,0:T(8,128)(2,1)}, u32[]{:S(2)}, u32[]{:S(2)}) collective-permute-start(bf16[928,512]{1,0:T(8,128)(2,1)S(1)} %slice.6.refs_0_), channel_id=1, source_target_pairs={{4,0},{8,4},{12,8},{0,12},{5,1},{9,5},{13,9},{1,13},{6,2},{10,6},{... | collective-permute-start | bytes 2850824 | tf_op jit(solution)/shard_map/ppermute | solution.py:19
  12.6 5.4 %collective-permute-start = (bf16[512,512]{1,0:T(8,128)(2,1)}, bf16[512,512]{1,0:T(8,128)(2,1)}, u32[]{:S(2)}, u32[]{:S(2)}) collective-permute-start(bf16[512,512]{1,0:T(8,128)(2,1)} %get-tuple-element.80), channel_id=1, source_target_pairs={{0,0},{1,1},{2,16},{3,17},{16,2},{17,3},{18,18},{19,19},{4,4},{5,5... | collective-permute-start | bytes 1572872 | tf_op jit(solution)/shard_map/ppermute | solution.py:307
  25.7 3.6 %shard_map.94 = bf16[128,512]{1,0:T(8,128)(2,1)S(1)} custom-call(s32[4]{0:T(128)S(1)} %gather_fusion, bf16[512,1024]{1,0:T(8,128)(2,1)S(1)} %copy-done.4, bf16[1848,512]{1,0:T(8,128)(2,1)S(1)} %bitcast.19, bf16[16,64,1024]{2,1,0:T(8,128)(2,1)S(1)} %copy-done.9, bf16[16,64,1848]{2,1,0:T(8,128)(2,1)S(1)} %copy-done.2), custom_call_target="tpu_custom_call" | custom-call | flops 1000000 | bytes 1000000 | tf_op jit(solution)/shard_map/pallas_call | solution.py:48
  29.4 2.6 %collective-permute-done.1 = bf16[512,512]{1,0:T(8,128)(2,1)} collective-permute-done((bf16[512,512]{1,0:T(8,128)(2,1)}, bf16[512,512]{1,0:T(8,128)(2,1)}, u32[]{:S(2)}, u32[]{:S(2)}) %collective-permute-start.1) | collective-permute-done | bytes 524320 | tf_op jit(solution)/shard_map/ppermute | solution.py:307
  31.9 3.3 %collective-permute-done.3.refs_3_ = bf16[928,512]{1,0:T(8,128)(2,1)S(1)} collective-permute-done((bf16[928,512]{1,0:T(8,128)(2,1)S(1)}, bf16[928,512]{1,0:T(8,128)(2,1)S(1)}, u32[]{:S(2)}, u32[]{:S(2)}) %collective-permute-start.3) | collective-permute-done | bytes 950304 | tf_op jit(solution)/shard_map/ppermute | solution.py:19
  35.2 2.6 %pad_maximum_fusion = bf16[2,512,512]{2,1,0:T(8,128)(2,1)} fusion(bf16[1,512,512]{2,1,0:T(8,128)(2,1)} %bitcast.6, bf16[1,512,512]{2,1,0:T(8,128)(2,1)} %bitcast.5), kind=kLoop, calls=%fused_computation.1 | loop fusion | flops 524288 | bytes 2097152 | tf_op jit(solution)/shard_map/stack | solution.py:317
  44.2 4.0 %collective-permute-done.5 = bf16[128,512]{1,0:T(8,128)(2,1)S(1)} collective-permute-done((bf16[128,512]{1,0:T(8,128)(2,1)S(1)}, bf16[128,512]{1,0:T(8,128)(2,1)S(1)}, u32[]{:S(2)}, u32[]{:S(2)}) %collective-permute-start.5) | collective-permute-done | bytes 131104 | tf_op jit(solution)/shard_map/ppermute | solution.py:28
  48.3 3.1 %collective-permute-start.6 = (bf16[128,512]{1,0:T(8,128)(2,1)S(1)}, bf16[128,512]{1,0:T(8,128)(2,1)S(1)}, u32[]{:S(2)}, u32[]{:S(2)}) collective-permute-start(bf16[128,512]{1,0:T(8,128)(2,1)S(1)} %add.53), channel_id=1, source_target_pairs={{0,96},{96,0},{32,64},{64,32},{1,97},{97,1},{33,65},{65,33},{2,98}... | collective-permute-start | bytes 393224 | tf_op jit(solution)/shard_map/ppermute | solution.py:29
  51.4 6.2 %collective-permute-done.6 = bf16[128,512]{1,0:T(8,128)(2,1)S(1)} collective-permute-done((bf16[128,512]{1,0:T(8,128)(2,1)S(1)}, bf16[128,512]{1,0:T(8,128)(2,1)S(1)}, u32[]{:S(2)}, u32[]{:S(2)}) %collective-permute-start.6) | collective-permute-done | bytes 131104 | tf_op jit(solution)/shard_map/ppermute | solution.py:29
  59.3 6.2 %shard_map.95 = (bf16[128,2944]{1,0:T(8,128)(2,1)}, bf16[128,2944]{1,0:T(8,128)(2,1)}, bf16[128,2944]{1,0:T(8,128)(2,1)S(1)}, bf16[128,2944]{1,0:T(8,128)(2,1)S(...) custom-call(s32[6]{0:T(128)S(1)} %pad_add_fusion.refs_0_, ...), custom_call_target="tpu_custom_call" | custom-call | flops 1000000 | bytes 1000000 | tf_op jit(solution)/shard_map/pallas_call | solution.py:48
  78.5 13.1 %collective-permute-done.18 = bf16[128,2944]{1,0:T(8,128)(2,1)} collective-permute-done((bf16[128,2944]{1,0:T(8,128)(2,1)}, bf16[128,2944]{1,0:T(8,128)(2,1)}, u32[]{:S(2)}, u32[]{:S(2)}) %collective-permute-start.18) | collective-permute-done | bytes 753696 | tf_op jit(solution)/shard_map/ppermute | solution.py:19
  91.6 2.4 %add.59 = bf16[128,2944]{1,0:T(8,128)(2,1)} add(bf16[128,2944]{1,0:T(8,128)(2,1)} %copy-done.12, bf16[128,2944]{1,0:T(8,128)(2,1)} %collective-permute-done.18) | non-fusion elementwise | flops 376832 | bytes 2260992 | tf_op jit(solution)/shard_map/add | solution.py:36
  99.9 3.4 %copy-done.1 = bf16[16,512,512]{2,1,0:T(8,128)(2,1)S(1)} copy-done((bf16[16,512,512]{2,1,0:T(8,128)(2,1)S(1)}, bf16[16,512,512]{2,1,0:T(8,128)(2,1)}, u32[]{:S(2)}) %copy-start.1) | copy-done | bytes 8388632
  103.3 6.9 %shard_map.97 = (bf16[928,512]{1,0:T(8,128)(2,1)S(1)}, bf16[928,512]{1,0:T(8,128)(2,1)S(1)}) custom-call(s32[3]{0:T(128)S(1)} %get-tuple-element.82.index, bf16[4,2,2,512,512]{4,3,2,1,0:T(8,128)(2,1)S(1)} %bitcast.13, bf16[928,512]{1,0:T(8,128)(2,1)S(1)} %slice.6.refs_0_, bf16[928,512]{1,0:T(8,128)(2,1)} %collective-permute-done.2.refs_1_, ...), custom_call_target="tpu_custom_call" | custom-call | flops 1000000 | bytes 1000000 | tf_op jit(solution)/shard_map/pallas_call | solution.py:48
  111.0 7.3 %shard_map.99 = (bf16[920,512]{1,0:T(8,128)(2,1)S(1)}, bf16[920,512]{1,0:T(8,128)(2,1)S(1)}) custom-call(s32[3]{0:T(128)S(1)} %get-tuple-element.84.index, bf16[4,2,2,512,512]{4,3,2,1,0:T(8,128)(2,1)S(1)} %bitcast.14, bf16[920,512]{1,0:T(8,128)(2,1)S(1)} %slice.7.refs_0_, bf16[920,512]{1,0:T(8,128)(2,1)} %collective-permute-done.7.refs_1_, ...), custom_call_target="tpu_custom_call" | custom-call | flops 1000000 | bytes 1000000 | tf_op jit(solution)/shard_map/pallas_call | solution.py:48
  118.4 2.7 %collective-permute-start.14 = (bf16[920,512]{1,0:T(8,128)(2,1)S(1)}, bf16[920,512]{1,0:T(8,128)(2,1)S(1)}, u32[]{:S(2)}, u32[]{:S(2)}) collective-permute-start(bf16[920,512]{1,0:T(8,128)(2,1)S(1)} %get-tuple-element.63), channel_id=1, source_target_pairs={{1,0},{2,1},{3,2},{0,3},{5,4},{6,5},{7,6},{4,7},{9,8},{10,9},{11,1... | collective-permute-start | bytes 2826248 | tf_op jit(solution)/shard_map/ppermute | solution.py:19
  121.1 8.0 %collective-permute-done.19.refs_2_ = bf16[128,2944]{1,0:T(8,128)(2,1)} collective-permute-done((bf16[128,2944]{1,0:T(8,128)(2,1)}, bf16[128,2944]{1,0:T(8,128)(2,1)}, u32[]{:S(2)}, u32[]{:S(2)}) %collective-permute-start.19) | collective-permute-done | bytes 753696 | tf_op jit(solution)/shard_map/ppermute | solution.py:19
  133.2 6.9 %shard_map.96 = (bf16[928,512]{1,0:T(8,128)(2,1)S(1)}, bf16[928,512]{1,0:T(8,128)(2,1)S(1)}) custom-call(s32[3]{0:T(128)S(1)} %get-tuple-element.81.index, bf16[4,2,2,512,512]{4,3,2,1,0:T(8,128)(2,1)S(1)} %bitcast.17, bf16[928,512]{1,0:T(8,128)(2,1)S(1)} %slice.6.refs_0_, bf16[928,512]{1,0:T(8,128)(2,1)} %collective-permute-done.2.refs_1_, ...), custom_call_target="tpu_custom_call" | custom-call | flops 1000000 | bytes 1000000 | tf_op jit(solution)/shard_map/pallas_call | solution.py:48
  140.2 5.3 %collective-permute-done.11 = bf16[928,512]{1,0:T(8,128)(2,1)S(1)} collective-permute-done((bf16[928,512]{1,0:T(8,128)(2,1)S(1)}, bf16[928,512]{1,0:T(8,128)(2,1)S(1)}, u32[]{:S(2)}, u32[]{:S(2)}) %collective-permute-start.11) | collective-permute-done | bytes 950304 | tf_op jit(solution)/shard_map/ppermute | solution.py:19
  147.2 6.9 %shard_map.98 = (bf16[920,512]{1,0:T(8,128)(2,1)S(1)}, bf16[920,512]{1,0:T(8,128)(2,1)S(1)}) custom-call(s32[3]{0:T(128)S(1)} %get-tuple-element.83.index, bf16[4,2,2,512,512]{4,3,2,1,0:T(8,128)(2,1)S(1)} %bitcast.18, bf16[920,512]{1,0:T(8,128)(2,1)S(1)} %slice.7.refs_0_, bf16[920,512]{1,0:T(8,128)(2,1)} %collective-permute-done.7.refs_1_, ...), custom_call_target="tpu_custom_call" | custom-call | flops 1000000 | bytes 1000000 | tf_op jit(solution)/shard_map/pallas_call | solution.py:48
  157.2 8.2 %collective-permute-done.24.before = bf16[64,2944]{1,0:T(8,128)(2,1)S(1)} collective-permute-done((bf16[64,2944]{1,0:T(8,128)(2,1)S(1)}, bf16[64,2944]{1,0:T(8,128)(2,1)S(1)}, u32[]{:S(2)}, u32[]{:S(2)}) %collective-permute-start.24) | collective-permute-done | bytes 376864 | tf_op jit(solution)/shard_map/ppermute | solution.py:19
  166.4 6.7 %collective-permute-done.25.after = bf16[64,2944]{1,0:T(8,128)(2,1)S(1)} collective-permute-done((bf16[64,2944]{1,0:T(8,128)(2,1)S(1)}, bf16[64,2944]{1,0:T(8,128)(2,1)S(1)}, u32[]{:S(2)}, u32[]{:S(2)}) %collective-permute-start.25) | collective-permute-done | bytes 376864 | tf_op jit(solution)/shard_map/ppermute | solution.py:19
  174.0 12.5 %collective-permute-done.16.refs_5_ = bf16[920,512]{1,0:T(8,128)(2,1)S(1)} collective-permute-done((bf16[920,512]{1,0:T(8,128)(2,1)S(1)}, bf16[920,512]{1,0:T(8,128)(2,1)S(1)}, u32[]{:S(2)}, u32[]{:S(2)}) %collective-permute-start.16) | collective-permute-done | bytes 942112 | tf_op jit(solution)/shard_map/ppermute | solution.py:19
  186.5 4.0 %shard_map.100 = bf16[1848,512]{1,0:T(8,128)(2,1)} custom-call(s32[4]{0:T(128)S(1)} %gather_fusion, bf16[128,512]{1,0:T(8,128)(2,1)S(1)} %add.54.refs_1_.summed, bf16[16,64,1848]{2,1,0:T(8,128)(2,1)S(1)} %copy-done.3, bf16[928,512]{1,0:T(8,128)(2,1)S(1)} %get-tuple-element.55.refs_0_, bf16[928,512]{1,0:T(8,128)(2,1)S(1)} %collective-permute-done.10.refs_1_, ...), custom_call_target="tpu_custom_call" | custom-call | flops 1000000 | bytes 1000000 | tf_op jit(solution)/shard_map/pallas_call | solution.py:48
  (100 shorter events, 48.8 us)
Async XLA Ops:
  7.2 92.7 %all-gather.3.cloned.1.call-start = ((), (), s32[]{:S(2)}) async-start(), calls=%async_computation | async-start | bytes 9437184 | tf_op jit(solution)/shard_map/all_gather | solution.py:317
  8.6 23.3 %collective-permute-start.2 = (bf16[928,512]{1,0:T(8,128)(2,1)S(1)}, bf16[928,512]{1,0:T(8,128)(2,1)}, u32[]{:S(2)}, u32[]{:S(2)}) collective-permute-start(bf16[928,512]{1,0:T(8,128)(2,1)S(1)} %slice.6.refs_0_), channel_id=1, source_target_pairs={{4,0},{8,4},{12,8},{0,12},{5,1},{9,5},{13,9},{1,13},{6,2},{10,6},{... | collective-permute-start | bytes 2850824 | tf_op jit(solution)/shard_map/ppermute | solution.py:19
  11.5 23.7 %collective-permute-start.3 = (bf16[928,512]{1,0:T(8,128)(2,1)S(1)}, bf16[928,512]{1,0:T(8,128)(2,1)S(1)}, u32[]{:S(2)}, u32[]{:S(2)}) collective-permute-start(bf16[928,512]{1,0:T(8,128)(2,1)S(1)} %slice.6.refs_0_), channel_id=1, source_target_pairs={{12,0},{0,4},{4,8},{8,12},{13,1},{1,5},{5,9},{9,13},{14,2},{2,6},{... | collective-permute-start | bytes 2850824 | tf_op jit(solution)/shard_map/ppermute | solution.py:19
  12.6 16.8 %collective-permute-start = (bf16[512,512]{1,0:T(8,128)(2,1)}, bf16[512,512]{1,0:T(8,128)(2,1)}, u32[]{:S(2)}, u32[]{:S(2)}) collective-permute-start(bf16[512,512]{1,0:T(8,128)(2,1)} %get-tuple-element.80), channel_id=1, source_target_pairs={{0,0},{1,1},{2,16},{3,17},{16,2},{17,3},{18,18},{19,19},{4,4},{5,5... | collective-permute-start | bytes 1572872 | tf_op jit(solution)/shard_map/ppermute | solution.py:307
  17.9 14.0 %collective-permute-start.1 = (bf16[512,512]{1,0:T(8,128)(2,1)}, bf16[512,512]{1,0:T(8,128)(2,1)}, u32[]{:S(2)}, u32[]{:S(2)}) collective-permute-start(bf16[512,512]{1,0:T(8,128)(2,1)} %get-tuple-element.79), channel_id=1, source_target_pairs={{0,1},{1,0},{2,17},{3,16},{16,3},{17,2},{18,19},{19,18},{4,5},{5,4... | collective-permute-start | bytes 1572872 | tf_op jit(solution)/shard_map/ppermute | solution.py:307
  39.1 30.8 %collective-permute-start.7 = (bf16[920,512]{1,0:T(8,128)(2,1)S(1)}, bf16[920,512]{1,0:T(8,128)(2,1)}, u32[]{:S(2)}, u32[]{:S(2)}) collective-permute-start(bf16[920,512]{1,0:T(8,128)(2,1)S(1)} %slice.7.refs_0_), channel_id=1, source_target_pairs={{4,0},{8,4},{12,8},{0,12},{5,1},{9,5},{13,9},{1,13},{6,2},{10,6},{... | collective-permute-start | bytes 2826248 | tf_op jit(solution)/shard_map/ppermute | solution.py:19
  39.6 30.4 %collective-permute-start.8 = (bf16[920,512]{1,0:T(8,128)(2,1)S(1)}, bf16[920,512]{1,0:T(8,128)(2,1)}, u32[]{:S(2)}, u32[]{:S(2)}) collective-permute-start(bf16[920,512]{1,0:T(8,128)(2,1)S(1)} %slice.7.refs_0_), channel_id=1, source_target_pairs={{12,0},{0,4},{4,8},{8,12},{13,1},{1,5},{5,9},{9,13},{14,2},{2,6},{... | collective-permute-start | bytes 2826248 | tf_op jit(solution)/shard_map/ppermute | solution.py:19
  48.3 9.4 %collective-permute-start.6 = (bf16[128,512]{1,0:T(8,128)(2,1)S(1)}, bf16[128,512]{1,0:T(8,128)(2,1)S(1)}, u32[]{:S(2)}, u32[]{:S(2)}) collective-permute-start(bf16[128,512]{1,0:T(8,128)(2,1)S(1)} %add.53), channel_id=1, source_target_pairs={{0,96},{96,0},{32,64},{64,32},{1,97},{97,1},{33,65},{65,33},{2,98}... | collective-permute-start | bytes 393224 | tf_op jit(solution)/shard_map/ppermute | solution.py:29
  70.0 28.5 %collective-permute-start.9 = (bf16[928,512]{1,0:T(8,128)(2,1)}, bf16[928,512]{1,0:T(8,128)(2,1)}, u32[]{:S(2)}, u32[]{:S(2)}) collective-permute-start(bf16[928,512]{1,0:T(8,128)(2,1)} %collective-permute-done.2.refs_1_), channel_id=1, source_target_pairs={{4,0},{8,4},{12,8},{0,12},{5,1},{9,5},{13,9},{1,13},{6,2},{10,6},{... | collective-permute-start | bytes 2850824 | tf_op jit(solution)/shard_map/ppermute | solution.py:19
  71.3 38.9 %collective-permute-start.13 = (bf16[920,512]{1,0:T(8,128)(2,1)}, bf16[920,512]{1,0:T(8,128)(2,1)}, u32[]{:S(2)}, u32[]{:S(2)}) collective-permute-start(bf16[920,512]{1,0:T(8,128)(2,1)} %collective-permute-done.8.refs_3_), channel_id=1, source_target_pairs={{12,0},{0,4},{4,8},{8,12},{13,1},{1,5},{5,9},{9,13},{14,2},{2,6},{... | collective-permute-start | bytes 2826248 | tf_op jit(solution)/shard_map/ppermute | solution.py:19
  72.0 19.6 %collective-permute-start.18 = (bf16[128,2944]{1,0:T(8,128)(2,1)}, bf16[128,2944]{1,0:T(8,128)(2,1)}, u32[]{:S(2)}, u32[]{:S(2)}) collective-permute-start(bf16[128,2944]{1,0:T(8,128)(2,1)} %get-tuple-element.68), channel_id=1, source_target_pairs={{3,0},{0,1},{1,2},{2,3},{7,4},{4,5},{5,6},{6,7},{11,8},{8,9},{9,10... | collective-permute-start | bytes 2261000 | tf_op jit(solution)/shard_map/ppermute | solution.py:19
  74.2 20.1 %collective-permute-start.20 = (bf16[128,2944]{1,0:T(8,128)(2,1)}, bf16[128,2944]{1,0:T(8,128)(2,1)}, u32[]{:S(2)}, u32[]{:S(2)}) collective-permute-start(bf16[128,2944]{1,0:T(8,128)(2,1)} %get-tuple-element.71), channel_id=1, source_target_pairs={{1,0},{2,1},{3,2},{0,3},{5,4},{6,5},{7,6},{4,7},{9,8},{10,9},{11,1... | collective-permute-start | bytes 2261000 | tf_op jit(solution)/shard_map/ppermute | solution.py:19
  76.4 41.9 %collective-permute-start.17 = (bf16[128,2944]{1,0:T(8,128)(2,1)}, bf16[128,2944]{1,0:T(8,128)(2,1)}, u32[]{:S(2)}, u32[]{:S(2)}) collective-permute-start(bf16[128,2944]{1,0:T(8,128)(2,1)} %get-tuple-element.66), channel_id=1, source_target_pairs={{1,0},{2,1},{3,2},{0,3},{5,4},{6,5},{7,6},{4,7},{9,8},{10,9},{11,1... | collective-permute-start | bytes 2261000 | tf_op jit(solution)/shard_map/ppermute | solution.py:19
  91.6 29.5 %collective-permute-start.22 = (bf16[128,2944]{1,0:T(8,128)(2,1)}, bf16[128,2944]{1,0:T(8,128)(2,1)}, u32[]{:S(2)}, u32[]{:S(2)}) collective-permute-start(bf16[128,2944]{1,0:T(8,128)(2,1)} %copy-done.17), channel_id=1, source_target_pairs={{3,0},{0,1},{1,2},{2,3},{7,4},{4,5},{5,6},{6,7},{11,8},{8,9},{9,10... | collective-permute-start | bytes 2261000 | tf_op jit(solution)/shard_map/ppermute | solution.py:19
  94.3 34.8 %collective-permute-start.19 = (bf16[128,2944]{1,0:T(8,128)(2,1)}, bf16[128,2944]{1,0:T(8,128)(2,1)}, u32[]{:S(2)}, u32[]{:S(2)}) collective-permute-start(bf16[128,2944]{1,0:T(8,128)(2,1)} %add.59), channel_id=1, source_target_pairs={{3,0},{0,1},{1,2},{2,3},{7,4},{4,5},{5,6},{6,7},{11,8},{8,9},{9,10... | collective-permute-start | bytes 2261000 | tf_op jit(solution)/shard_map/ppermute | solution.py:19
  98.5 30.6 %collective-permute-start.21 = (bf16[128,2944]{1,0:T(8,128)(2,1)}, bf16[128,2944]{1,0:T(8,128)(2,1)}, u32[]{:S(2)}, u32[]{:S(2)}) collective-permute-start(bf16[128,2944]{1,0:T(8,128)(2,1)} %add.60), channel_id=1, source_target_pairs={{1,0},{2,1},{3,2},{0,3},{5,4},{6,5},{7,6},{4,7},{9,8},{10,9},{11,1... | collective-permute-start | bytes 2261000 | tf_op jit(solution)/shard_map/ppermute | solution.py:19
  110.2 35.3 %collective-permute-start.11 = (bf16[928,512]{1,0:T(8,128)(2,1)S(1)}, bf16[928,512]{1,0:T(8,128)(2,1)S(1)}, u32[]{:S(2)}, u32[]{:S(2)}) collective-permute-start(bf16[928,512]{1,0:T(8,128)(2,1)S(1)} %get-tuple-element.58), channel_id=1, source_target_pairs={{3,0},{0,1},{1,2},{2,3},{7,4},{4,5},{5,6},{6,7},{11,8},{8,9},{9,10... | collective-permute-start | bytes 2850824 | tf_op jit(solution)/shard_map/ppermute | solution.py:19
  118.4 35.8 %collective-permute-start.14 = (bf16[920,512]{1,0:T(8,128)(2,1)S(1)}, bf16[920,512]{1,0:T(8,128)(2,1)S(1)}, u32[]{:S(2)}, u32[]{:S(2)}) collective-permute-start(bf16[920,512]{1,0:T(8,128)(2,1)S(1)} %get-tuple-element.63), channel_id=1, source_target_pairs={{1,0},{2,1},{3,2},{0,3},{5,4},{6,5},{7,6},{4,7},{9,8},{10,9},{11,1... | collective-permute-start | bytes 2826248 | tf_op jit(solution)/shard_map/ppermute | solution.py:19
  131.4 25.2 %collective-permute-start.23 = (bf16[64,2944]{1,0:T(8,128)(2,1)S(1)}, bf16[64,2944]{1,0:T(8,128)(2,1)S(1)}, u32[]{:S(2)}, u32[]{:S(2)}) collective-permute-start(bf16[64,2944]{1,0:T(8,128)(2,1)S(1)} %get-tuple-element.74), channel_id=1, source_target_pairs={{8,0},{12,4},{0,8},{4,12},{9,1},{13,5},{1,9},{5,13},{10,2},{14,6},... | collective-permute-start | bytes 1130504 | tf_op jit(solution)/shard_map/ppermute | solution.py:19
  132.4 54.1 %collective-permute-start.10 = (bf16[928,512]{1,0:T(8,128)(2,1)S(1)}, bf16[928,512]{1,0:T(8,128)(2,1)S(1)}, u32[]{:S(2)}, u32[]{:S(2)}) collective-permute-start(bf16[928,512]{1,0:T(8,128)(2,1)S(1)} %get-tuple-element.56), channel_id=1, source_target_pairs={{1,0},{2,1},{3,2},{0,3},{5,4},{6,5},{7,6},{4,7},{9,8},{10,9},{11,1... | collective-permute-start | bytes 2850824 | tf_op jit(solution)/shard_map/ppermute | solution.py:19
  145.8 40.7 %collective-permute-start.12 = (bf16[928,512]{1,0:T(8,128)(2,1)S(1)}, bf16[928,512]{1,0:T(8,128)(2,1)S(1)}, u32[]{:S(2)}, u32[]{:S(2)}) collective-permute-start(bf16[928,512]{1,0:T(8,128)(2,1)S(1)} %add.57), channel_id=1, source_target_pairs={{3,0},{0,1},{1,2},{2,3},{7,4},{4,5},{5,6},{6,7},{11,8},{8,9},{9,10... | collective-permute-start | bytes 2850824 | tf_op jit(solution)/shard_map/ppermute | solution.py:19
  145.9 40.6 %collective-permute-start.16 = (bf16[920,512]{1,0:T(8,128)(2,1)S(1)}, bf16[920,512]{1,0:T(8,128)(2,1)S(1)}, u32[]{:S(2)}, u32[]{:S(2)}) collective-permute-start(bf16[920,512]{1,0:T(8,128)(2,1)S(1)} %get-tuple-element.64), channel_id=1, source_target_pairs={{3,0},{0,1},{1,2},{2,3},{7,4},{4,5},{5,6},{6,7},{11,8},{8,9},{9,10... | collective-permute-start | bytes 2826248 | tf_op jit(solution)/shard_map/ppermute | solution.py:19
  154.4 32.1 %collective-permute-start.15 = (bf16[920,512]{1,0:T(8,128)(2,1)S(1)}, bf16[920,512]{1,0:T(8,128)(2,1)S(1)}, u32[]{:S(2)}, u32[]{:S(2)}) collective-permute-start(bf16[920,512]{1,0:T(8,128)(2,1)S(1)} %add.58), channel_id=1, source_target_pairs={{1,0},{2,1},{3,2},{0,3},{5,4},{6,5},{7,6},{4,7},{9,8},{10,9},{11,1... | collective-permute-start | bytes 2826248 | tf_op jit(solution)/shard_map/ppermute | solution.py:19
  156.7 8.8 %collective-permute-start.24 = (bf16[64,2944]{1,0:T(8,128)(2,1)S(1)}, bf16[64,2944]{1,0:T(8,128)(2,1)S(1)}, u32[]{:S(2)}, u32[]{:S(2)}) collective-permute-start(bf16[64,2944]{1,0:T(8,128)(2,1)S(1)} %get-tuple-element.75), channel_id=1, source_target_pairs={{12,0},{0,4},{4,8},{8,12},{13,1},{1,5},{5,9},{9,13},{14,2},{2,6},{... | collective-permute-start | bytes 1130504 | tf_op jit(solution)/shard_map/ppermute | solution.py:19
  (24 other events, 213.8 us)
Sparse Core Ops, SparseCore 0:
  38.0 51.9 all-gather.2

commit v2 on v1

--- a/solution.py
+++ b/solution.py
@@ -10,6 +10,7 @@
 adapter_scale = 2.0
 N = 4
 MIB = 1024 * 1024
+BIG = 52
 NN = (((1,), (0,)), ((), ()))
 NT = (((1,), (1,)), ((), ()))
 TN = (((0,), (0,)), ((), ()))
@@ -106,61 +107,65 @@
             pltpu.VMEM((blocks, rank, units), jnp.bfloat16),
             pltpu.SemaphoreType.DMA((2 + 2 * blocks,)),
         ],
-        8,
-    )
-
-
-def terms_kernel(multiplier, index, summed, cotangent, hidden, *refs):
-    outs, products = refs[:8], refs[8]
-    blocks = products.shape[0]
-    rows = cotangent.shape[0] // blocks
-    width = cotangent.shape[1]
+        BIG,
+    )
+
+
+def gradient_terms(index, summed, cotangent, hidden, multiplier):
+    blocks = index.shape[0] - 1
+    tokens, width = cotangent.shape
+    rows = tokens // blocks
     units = hidden.shape[0]
-    rank = summed.shape[0] // 2
-    for b in range(blocks):
-        at = slice(b * rows, (b + 1) * rows)
-        products[b, :, :width] = lax.dot_general(
-            summed[rank:, at], cotangent[at, :], NN, preferred_element_type=jnp.float32
-        )
-        products[b, :, width : width + units] = lax.dot_general(
-            summed[:rank, at], hidden[:, at], NT, preferred_element_type=jnp.float32
-        )
-        products[b, :, width + units :] = jnp.zeros(
-            (rank, products.shape[2] - width - units), jnp.float32
-        )
-    x, z = index[blocks], index[blocks + 1]
-    for place, s in enumerate((2, 1, 3, 0)):
-        for part, t in enumerate((2, 1, 3, 0)):
-            slot = lax.rem(x + t, N) * N + lax.rem(z + s, N)
-            total = jnp.zeros(products.shape[1:], jnp.float32)
-            for b in range(blocks):
-                weight = jnp.where(index[b] == slot, jnp.float32(multiplier), jnp.float32(0))
-                total = total + weight * products[b]
-            ref = outs[place * 2 + part // 2]
-            row = part % 2 * rank
-            ref[row : row + rank, :] = total.astype(ref.dtype)
-
-
-def gradient_terms(index, summed, cotangent, hidden, multiplier):
-    blocks = index.shape[0] - 2
-    wide = cotangent.shape[1] + hidden.shape[0]
+    wide = width + units
     wide = wide + -wide % 128
     rank = summed.shape[0] // 2
-    shape = (2 * rank, wide)
-
-    def kernel(*refs):
-        terms_kernel(multiplier, *refs)
+    shape = (N, N * rank, wide)
+
+    def kernel(index, summed, cotangent, hidden, out, products, staged, sems):
+        for b in range(blocks):
+            at = slice(b * rows, (b + 1) * rows)
+            products[b, :, :width] = lax.dot_general(
+                summed[rank:, at], cotangent[at, :], NN, preferred_element_type=jnp.float32
+            )
+            products[b, :, width : width + units] = lax.dot_general(
+                summed[:rank, at], hidden[:, at], NT, preferred_element_type=jnp.float32
+            )
+            products[b, :, width + units :] = jnp.zeros((rank, wide - width - units), jnp.float32)
+        x = index[blocks]
+        copies = []
+        for s in range(N):
+            for t in range(N):
+                slot = lax.rem(x + t, N) * N + s
+                total = jnp.zeros((rank, wide), jnp.float32)
+                for b in range(blocks):
+                    weight = jnp.where(index[b] == slot, jnp.float32(multiplier), jnp.float32(0))
+                    total = total + weight * products[b]
+                staged[s, t * rank : (t + 1) * rank, :] = total.astype(staged.dtype)
+            copies.append(pltpu.make_async_copy(staged.at[s], out.at[s], sems.at[s]))
+            copies[s].start()
+        for copy in copies:
+            copy.wait()
 
     return call(
         kernel,
         (1,),
         (index, summed, cotangent, hidden),
         [whole(a) for a in (summed, cotangent, hidden)],
-        [pl.BlockSpec(memory_space=pltpu.VMEM)] * 8,
-        [jax.ShapeDtypeStruct(shape, jnp.bfloat16)] * 8,
-        [pltpu.VMEM((blocks, rank, wide), jnp.float32)],
-        20,
-    )
+        pl.BlockSpec(memory_space=pl.ANY),
+        jax.ShapeDtypeStruct(shape, jnp.bfloat16),
+        [
+            pltpu.VMEM((blocks, rank, wide), jnp.float32),
+            pltpu.VMEM(shape, jnp.bfloat16),
+            pltpu.SemaphoreType.DMA((N,)),
+        ],
+        BIG,
+    )
+
+
+def second_hop(sums, axis):
+    rank = sums.shape[0] // N
+    parts = [sums[t * rank : (t + 1) * rank] for t in range(N)]
+    return [parts[0]] + [take_from(parts[t], axis, -t) for t in range(1, N)]
 
 
 def added(refs, at):
@@ -168,26 +173,6 @@
     for ref in refs[1:]:
         total = total + ref[at, :].astype(jnp.float32)
     return total
-
-
-def middle_kernel(*refs):
-    outs = refs[6:]
-    rank = outs[0].shape[0]
-    for n, out in enumerate(outs):
-        at = slice(n % 2 * rank, (n % 2 + 1) * rank)
-        out[...] = added(refs[n // 2 * 3 : n // 2 * 3 + 3], at).astype(out.dtype)
-
-
-def middle_sums(lows, highs):
-    rows, wide = lows[0].shape
-    shape = (rows // 2, wide)
-    kinds = [jnp.bfloat16] * 3 + [jnp.float32]
-    return pl.pallas_call(
-        middle_kernel,
-        out_shape=[jax.ShapeDtypeStruct(shape, kind) for kind in kinds],
-        compiler_params=pltpu.CompilerParams(vmem_limit_bytes=10 * MIB),
-        cost_estimate=pl.CostEstimate(flops=1000000, bytes_accessed=1000000, transcendentals=0),
-    )(*lows, *highs)
 
 
 def last_kernel(own, across, before, after, out_in, out_out):
@@ -205,6 +190,24 @@
         compiler_params=pltpu.CompilerParams(vmem_limit_bytes=6 * MIB),
         cost_estimate=pl.CostEstimate(flops=1000000, bytes_accessed=1000000, transcendentals=0),
     )(*parts)
+
+
+def packed(pieces):
+    rows, width = pieces[0].shape
+
+    def kernel(*refs):
+        for n, ref in enumerate(refs[:-1]):
+            refs[-1][n] = ref[...]
+
+    return pl.pallas_call(
+        kernel,
+        grid=(2,),
+        in_specs=[pl.BlockSpec((rows // 2, width), lambda i: (i, 0))] * len(pieces),
+        out_specs=pl.BlockSpec((len(pieces), rows // 2, width), lambda i: (0, i, 0)),
+        out_shape=jax.ShapeDtypeStruct((len(pieces), rows, width), pieces[0].dtype),
+        compiler_params=pltpu.CompilerParams(vmem_limit_bytes=BIG * MIB),
+        cost_estimate=pl.CostEstimate(flops=1000000, bytes_accessed=1000000, transcendentals=0),
+    )(*pieces)
 
 
 def products(index, gathered, weights, steps):
@@ -250,7 +253,7 @@
             pltpu.VMEM((2, N, tokens, width), jnp.bfloat16),
             pltpu.SemaphoreType.DMA((3, N)),
         ],
-        20,
+        BIG,
     )
 
 
@@ -285,7 +288,7 @@
         pl.BlockSpec((units, rows), lambda i, s: (0, i)),
         jax.ShapeDtypeStruct((units, tokens), jnp.bfloat16),
         [],
-        10,
+        BIG,
     )
 
 
@@ -307,21 +310,20 @@
         turned.append(lax.ppermute(piece, ("c", "z"), pairs))
     first = (units // 2 + 15) // 16 * 16
     own = [down_weight[:first], down_weight[first:]]
-    after = [take_from(p, "x", 1) for p in own]
-    before = [take_from(p, "x", -1) for p in own]
-
-    ranks = rank_sums(slots, cotangent, hidden, adapter_out, adapter_in)
-    turned[0], turned[1], after[0], before[0], ranks = lax.optimization_barrier(
-        (turned[0], turned[1], after[0], before[0], ranks)
-    )
-    gathered = lax.all_gather(jnp.stack(turned), ("y", "c"))
-    gathered = gathered.reshape(N, 2, 2, tokens, width)
-    summed = sum_over_dp(ranks)
-    index = jnp.concatenate([slots, jnp.stack([x, z]).astype(jnp.int32)])
+    after, before = [take_from(own[0], "x", 1)], [take_from(own[0], "x", -1)]
+
+    barrier = lax.optimization_barrier
+    summed = sum_over_dp(rank_sums(slots, cotangent, hidden, adapter_out, adapter_in))
+    *turned, after[0], before[0], summed, own[1] = barrier(
+        (*turned, after[0], before[0], summed, own[1])
+    )
+    gathered = lax.all_gather(packed(turned), ("y", "c")).reshape(N, 2, 2, tokens, width)
+    after.append(take_from(own[1], "x", 1))
+    before.append(take_from(own[1], "x", -1))
+    index = jnp.concatenate([slots, x[None].astype(jnp.int32)])
     terms = gradient_terms(index, summed, cotangent, hidden, adapter_scale / math.sqrt(tokens))
-    after[0], after[1], before[1], *terms = lax.optimization_barrier(
-        (after[0], after[1], before[1], *terms)
-    )
+    sums = lax.psum_scatter(terms, "z", scatter_dimension=0)
+    after[0], after[1], before[1], terms = barrier((after[0], after[1], before[1], terms))
     fars = [take_from(after[0], "x", 1), take_from(before[1], "x", -1)]
 
     def make(chunk, *steps):
@@ -337,11 +339,7 @@
     parts += scatter_ring(far1, right1, left1, own1, "z", -1)
     hidden_gradient = finish(slots, summed, adapter_in, parts)
 
-    lows = scatter_ring(*terms[0::2], "z", 1)
-    highs = scatter_ring(*terms[1::2], "z", -1)
-    across, before, after, own = middle_sums(lows, highs)
-    others = [take_from(p, "x", s) for p, s in ((across, 2), (before, -1), (after, 1))]
-    grad_in, grad_out = last_sum([own] + others, units, cotangent.shape[1])
+    grad_in, grad_out = last_sum(second_hop(sums, "x"), units, cotangent.shape[1])
     return hidden_gradient.T, grad_in, grad_out
 
 

time: 199 us -> 189 us (0.950)
  local copies, waits for them, and re-layouts: 19 us -> 12.3 us
  other arithmetic: 8.1 us -> 2.04 us
  Pallas kernels: 45.2 us -> 49.5 us
  starting transfers between devices: 39.3 us -> 35.3 us
    ppermute x21 -> x15, waiting for transfers between devices: 57.5 us -> 67.2 us  [take_from(): return lax.ppermute(array, axis, [((i + step) % N, i) for i in range(N)])]
    unnamed x42 -> x24, local copies, waits for them, and re-layouts: 14.7 us -> 5.62 us
    pallas_call x7, Pallas kernels: 42 us -> 47.6 us  [call(): pl.pallas_call(kernel, grid_spec=pltpu.PrefetchScalarGridSpec(num_scalar_...]
    ppermute x1, waiting for transfers between devices: 6.19 us -> 1.11 us  [sum_over_dp(): return array + lax.ppermute(array, 'y', [(0, 3), (3, 0), (1, 2), (2, 1)])]
    ppermute x2, starting transfers between devices: 7.28 us -> 3.6 us  [body(): turned.append(lax.ppermute(piece, ('c', 'z'), pairs))]
    ppermute x21 -> x15, starting transfers between devices: 27.2 us -> 24.2 us  [take_from(): return lax.ppermute(array, axis, [((i + step) % N, i) for i in range(N)])]
    ppermute x1, starting transfers between devices: 0.01 us -> 2.63 us  [other_core(): return lax.ppermute(array, 'c', [(0, 1), (1, 0)])]
    another operation x1 -> x0, other arithmetic: 2.61 us -> none  [body(): gathered = lax.all_gather(jnp.stack(turned), ('y', 'c'))]
  transfers between devices with their start and end apart: 27 -> 22, of which waited for: 12 -> 10; matrix products, arithmetic and copies ran while one was open for 4% -> 4% of each run, Pallas kernels for 21% -> 23%
where the time goes in v2:
time: 189 us; the launch traced here: 188 us
  waiting for transfers between devices  73.5 us (39%)
  Pallas kernels  49.5 us (26%)
  starting transfers between devices  35.3 us (19%)
  between operations  15.7 us (8%)
  local copies, waits for them, and re-layouts  12.3 us (7%)
  other arithmetic  2.04 us (1%)
    ppermute x15, waiting for transfers between devices, take_from(): return lax.ppermute(array, axis, [((i + step) % N, i) for i in range(N)])  67.2 us
    pallas_call x7, Pallas kernels, call(): pl.pallas_call(kernel, grid_spec=pltpu.PrefetchScalarGridSpec(num_scalar_...  47.6 us
    ppermute x15, starting transfers between devices, take_from(): return lax.ppermute(array, axis, [((i + step) % N, i) for i in range(N)])  24.2 us
    unnamed x24, local copies, waits for them, and re-layouts  5.62 us
    ppermute x1, waiting for transfers between devices, sum_over_dp(): array = array + lax.ppermute(array, 'y', [(0, 1), (1, 0), (2, 3), (3, 2)])  4.17 us
  transfers between devices with their start and end apart: 22, of which 10 were waited for; matrix products, arithmetic and copies ran while one was open for 4% of the time, Pallas kernels for 23%

profile of v2, /device:TPU:0, one launch (start us, length us, event | category | flops | bytes accessed | tf_op | source)
XLA Modules:
  0.0 188.4 jit_solution(4023890504368055551)
XLA Ops:
  9.4 2.9 %collective-permute-start.2 = (bf16[928,512]{1,0:T(8,128)(2,1)S(1)}, bf16[928,512]{1,0:T(8,128)(2,1)}, u32[]{:S(2)}, u32[]{:S(2)}) collective-permute-start(bf16[928,512]{1,0:T(8,128)(2,1)S(1)} %slice.30.refs_0_), channel_id=1, source_target_pairs={{4,0},{8,4},{12,8},{0,12},{5,1},{9,5},{13,9},{1,13},{6,2},{10,6},{... | collective-permute-start | bytes 2850824 | tf_op jit(solution)/shard_map/ppermute | solution.py:20
  17.7 3.3 %shard_map.94 = bf16[128,512]{1,0:T(8,128)(2,1)S(1)} custom-call(s32[4]{0:T(128)S(1)} %gather_fusion, bf16[512,1024]{1,0:T(8,128)(2,1)S(1)} %copy-done.1, bf16[1848,512]{1,0:T(8,128)(2,1)} %bitcast.22, bf16[16,64,1024]{2,1,0:T(8,128)(2,1)} %a_out.1, bf16[16,64,1848]{2,1,0:T(8,128)(2,1)} %a_in.3), custom_call_target="tpu_custom_call" | custom-call | flops 1000000 | bytes 1000000 | tf_op jit(solution)/shard_map/pallas_call | solution.py:49
  21.0 2.6 %collective-permute-start.4 = (bf16[128,512]{1,0:T(8,128)(2,1)S(1)}, bf16[128,512]{1,0:T(8,128)(2,1)S(1)}, u32[]{:S(2)}, u32[]{:S(2)}) collective-permute-start(bf16[128,512]{1,0:T(8,128)(2,1)S(1)} %shard_map.94), channel_id=1, source_target_pairs={{0,16},{16,0},{1,17},{17,1},{2,18},{18,2},{3,19},{19,3},{4,20},{20... | collective-permute-start | bytes 393224 | tf_op jit(solution)/shard_map/ppermute | solution.py:24
  26.4 4.2 %collective-permute-done.5 = bf16[128,512]{1,0:T(8,128)(2,1)S(1)} collective-permute-done((bf16[128,512]{1,0:T(8,128)(2,1)S(1)}, bf16[128,512]{1,0:T(8,128)(2,1)S(1)}, u32[]{:S(2)}, u32[]{:S(2)}) %collective-permute-start.5) | collective-permute-done | bytes 131104 | tf_op jit(solution)/shard_map/ppermute | solution.py:29
  30.6 3.1 %collective-permute-start.6 = (bf16[128,512]{1,0:T(8,128)(2,1)S(1)}, bf16[128,512]{1,0:T(8,128)(2,1)S(1)}, u32[]{:S(2)}, u32[]{:S(2)}) collective-permute-start(bf16[128,512]{1,0:T(8,128)(2,1)S(1)} %add.49), channel_id=1, source_target_pairs={{0,96},{96,0},{32,64},{64,32},{1,97},{97,1},{33,65},{65,33},{2,98}... | collective-permute-start | bytes 393224 | tf_op jit(solution)/shard_map/ppermute | solution.py:30
  33.7 2.2 %slice.31.refs_0_ = bf16[920,512]{1,0:T(8,128)(2,1)} slice(bf16[1848,512]{1,0:T(8,128)(2,1)} %param.9), slice={[928:1848], [0:512]} | slice | bytes 1884160 | tf_op jit(solution)/shard_map/slice | solution.py:312
  38.2 8.8 %shard_map.96 = bf16[4,256,2944]{2,1,0:T(8,128)(2,1)} custom-call(s32[5]{0:T(128)S(1)} %pad_add_fusion.index, bf16[128,512]{1,0:T(8,128)(2,1)S(1)} %add.50.summed, bf16[512,1024]{1,0:T(8,128)(2,1)S(1)} %copy-done.1, bf16[1848,512]{1,0:T(8,128)(2,1)} %bitcast.23), custom_call_target="tpu_custom_call" | custom-call | flops 1000000 | bytes 1000000 | tf_op jit(solution)/shard_map/pallas_call | solution.py:49
  48.3 3.2 %collective-permute-start.7 = (bf16[920,512]{1,0:T(8,128)(2,1)S(1)}, bf16[920,512]{1,0:T(8,128)(2,1)S(1)}, u32[]{:S(2)}, u32[]{:S(2)}) collective-permute-start(bf16[920,512]{1,0:T(8,128)(2,1)S(1)} %copy-done.4), channel_id=1, source_target_pairs={{4,0},{8,4},{12,8},{0,12},{5,1},{9,5},{13,9},{1,13},{6,2},{10,6},{... | collective-permute-start | bytes 2826248 | tf_op jit(solution)/shard_map/ppermute | solution.py:20
  51.6 19.0 %collective-permute-done.7.refs_1_ = bf16[920,512]{1,0:T(8,128)(2,1)S(1)} collective-permute-done((bf16[920,512]{1,0:T(8,128)(2,1)S(1)}, bf16[920,512]{1,0:T(8,128)(2,1)S(1)}, u32[]{:S(2)}, u32[]{:S(2)}) %collective-permute-start.7) | collective-permute-done | bytes 942112 | tf_op jit(solution)/shard_map/ppermute | solution.py:20
  71.6 2.6 %collective-permute-done.8.refs_3_ = bf16[920,512]{1,0:T(8,128)(2,1)} collective-permute-done((bf16[920,512]{1,0:T(8,128)(2,1)S(1)}, bf16[920,512]{1,0:T(8,128)(2,1)}, u32[]{:S(2)}, u32[]{:S(2)}) %collective-permute-start.8) | collective-permute-done | bytes 942112 | tf_op jit(solution)/shard_map/ppermute | solution.py:20
  76.2 18.6 %collective-permute-done.9.refs_2_ = bf16[928,512]{1,0:T(8,128)(2,1)S(1)} collective-permute-done((bf16[928,512]{1,0:T(8,128)(2,1)}, bf16[928,512]{1,0:T(8,128)(2,1)S(1)}, u32[]{:S(2)}, u32[]{:S(2)}) %collective-permute-start.9) | collective-permute-done | bytes 950304 | tf_op jit(solution)/shard_map/ppermute | solution.py:20
  95.8 7.2 %shard_map.98 = (bf16[928,512]{1,0:T(8,128)(2,1)S(1)}, bf16[928,512]{1,0:T(8,128)(2,1)S(1)}) custom-call(s32[3]{0:T(128)S(1)} %get-tuple-element.48.index, bf16[4,2,2,512,512]{4,3,2,1,0:T(8,128)(2,1)} %bitcast.18, bf16[928,512]{1,0:T(8,128)(2,1)} %copy-done.3, bf16[928,512]{1,0:T(8,128)(2,1)} %collective-permute-done.2.refs_1_, bf16[928,512]{1,0:T(8,128)(2,1)} %copy-done.5, ...), custom_call_target="tpu_custom_call" | custom-call | flops 1000000 | bytes 1000000 | tf_op jit(solution)/shard_map/pallas_call | solution.py:49
  105.0 8.2 %shard_map.100 = (bf16[920,512]{1,0:T(8,128)(2,1)}, bf16[920,512]{1,0:T(8,128)(2,1)}) custom-call(s32[3]{0:T(128)S(1)} %get-tuple-element.50.index, bf16[4,2,2,512,512]{4,3,2,1,0:T(8,128)(2,1)} %bitcast.19, bf16[920,512]{1,0:T(8,128)(2,1)} %slice.31.refs_0_, bf16[920,512]{1,0:T(8,128)(2,1)} %copy-done.6, bf16[920,512]{1,0:T(8,128)(2,1)} %copy-done.7, ...), custom_call_target="tpu_custom_call" | custom-call | flops 1000000 | bytes 1000000 | tf_op jit(solution)/shard_map/pallas_call | solution.py:49
  113.3 2.3 %collective-permute-start.14 = (bf16[920,512]{1,0:T(8,128)(2,1)}, bf16[920,512]{1,0:T(8,128)(2,1)S(1)}, u32[]{:S(2)}, u32[]{:S(2)}) collective-permute-start(bf16[920,512]{1,0:T(8,128)(2,1)} %get-tuple-element.37), channel_id=1, source_target_pairs={{1,0},{2,1},{3,2},{0,3},{5,4},{6,5},{7,6},{4,7},{9,8},{10,9},{11,1... | collective-permute-start | bytes 2826248 | tf_op jit(solution)/shard_map/ppermute | solution.py:20
  119.9 7.2 %shard_map.97 = (bf16[928,512]{1,0:T(8,128)(2,1)S(1)}, bf16[928,512]{1,0:T(8,128)(2,1)S(1)}) custom-call(s32[3]{0:T(128)S(1)} %get-tuple-element.47.index, bf16[4,2,2,512,512]{4,3,2,1,0:T(8,128)(2,1)} %bitcast.20, bf16[928,512]{1,0:T(8,128)(2,1)} %copy-done.3, bf16[928,512]{1,0:T(8,128)(2,1)} %collective-permute-done.2.refs_1_, bf16[928,512]{1,0:T(8,128)(2,1)} %copy-done.5, ...), custom_call_target="tpu_custom_call" | custom-call | flops 1000000 | bytes 1000000 | tf_op jit(solution)/shard_map/pallas_call | solution.py:49
  127.1 2.0 %collective-permute-done.11 = bf16[928,512]{1,0:T(8,128)(2,1)} collective-permute-done((bf16[928,512]{1,0:T(8,128)(2,1)S(1)}, bf16[928,512]{1,0:T(8,128)(2,1)}, u32[]{:S(2)}, u32[]{:S(2)}) %collective-permute-start.11) | collective-permute-done | bytes 950304 | tf_op jit(solution)/shard_map/ppermute | solution.py:20
  131.3 7.2 %shard_map.99 = (bf16[920,512]{1,0:T(8,128)(2,1)S(1)}, bf16[920,512]{1,0:T(8,128)(2,1)S(1)}) custom-call(s32[3]{0:T(128)S(1)} %get-tuple-element.49.index, bf16[4,2,2,512,512]{4,3,2,1,0:T(8,128)(2,1)} %bitcast.21, bf16[920,512]{1,0:T(8,128)(2,1)} %slice.31.refs_0_, bf16[920,512]{1,0:T(8,128)(2,1)} %copy-done.6, bf16[920,512]{1,0:T(8,128)(2,1)} %copy-done.7, ...), custom_call_target="tpu_custom_call" | custom-call | flops 1000000 | bytes 1000000 | tf_op jit(solution)/shard_map/pallas_call | solution.py:49
  138.8 3.0 %collective-permute-start.15 = (bf16[920,512]{1,0:T(8,128)(2,1)S(1)}, bf16[920,512]{1,0:T(8,128)(2,1)S(1)}, u32[]{:S(2)}, u32[]{:S(2)}) collective-permute-start(bf16[920,512]{1,0:T(8,128)(2,1)S(1)} %add.54), channel_id=1, source_target_pairs={{1,0},{2,1},{3,2},{0,3},{5,4},{6,5},{7,6},{4,7},{9,8},{10,9},{11,1... | collective-permute-start | bytes 2826248 | tf_op jit(solution)/shard_map/ppermute | solution.py:20
  141.7 3.0 %collective-permute-start.18 = (bf16[64,2944]{1,0:T(8,128)(2,1)S(1)}, bf16[64,2944]{1,0:T(8,128)(2,1)S(1)}, u32[]{:S(2)}, u32[]{:S(2)}) collective-permute-start(bf16[64,2944]{1,0:T(8,128)(2,1)S(1)} %get-tuple-element.42), channel_id=1, source_target_pairs={{8,0},{12,4},{0,8},{4,12},{9,1},{13,5},{1,9},{5,13},{10,2},{14,6},... | collective-permute-start | bytes 1130504 | tf_op jit(solution)/shard_map/ppermute | solution.py:20
  144.7 7.3 %collective-permute-done.18.before = bf16[64,2944]{1,0:T(8,128)(2,1)S(1)} collective-permute-done((bf16[64,2944]{1,0:T(8,128)(2,1)S(1)}, bf16[64,2944]{1,0:T(8,128)(2,1)S(1)}, u32[]{:S(2)}, u32[]{:S(2)}) %collective-permute-start.18) | collective-permute-done | bytes 376864 | tf_op jit(solution)/shard_map/ppermute | solution.py:20
  152.0 3.1 %collective-permute-start.19 = (bf16[64,2944]{1,0:T(8,128)(2,1)S(1)}, bf16[64,2944]{1,0:T(8,128)(2,1)S(1)}, u32[]{:S(2)}, u32[]{:S(2)}) collective-permute-start(bf16[64,2944]{1,0:T(8,128)(2,1)S(1)} %get-tuple-element.41), channel_id=1, source_target_pairs={{4,0},{8,4},{12,8},{0,12},{5,1},{9,5},{13,9},{1,13},{6,2},{10,6},{... | collective-permute-start | bytes 1130504 | tf_op jit(solution)/shard_map/ppermute | solution.py:20
  155.1 5.2 %collective-permute-done.19.after = bf16[64,2944]{1,0:T(8,128)(2,1)S(1)} collective-permute-done((bf16[64,2944]{1,0:T(8,128)(2,1)S(1)}, bf16[64,2944]{1,0:T(8,128)(2,1)S(1)}, u32[]{:S(2)}, u32[]{:S(2)}) %collective-permute-start.19) | collective-permute-done | bytes 376864 | tf_op jit(solution)/shard_map/ppermute | solution.py:20
  161.2 12.5 %collective-permute-done.16.refs_5_ = bf16[920,512]{1,0:T(8,128)(2,1)S(1)} collective-permute-done((bf16[920,512]{1,0:T(8,128)(2,1)}, bf16[920,512]{1,0:T(8,128)(2,1)S(1)}, u32[]{:S(2)}, u32[]{:S(2)}) %collective-permute-start.16) | collective-permute-done | bytes 942112 | tf_op jit(solution)/shard_map/ppermute | solution.py:20
  175.3 5.7 %shard_map.101 = bf16[1848,512]{1,0:T(8,128)(2,1)} custom-call(s32[4]{0:T(128)S(1)} %gather_fusion, bf16[128,512]{1,0:T(8,128)(2,1)S(1)} %add.50.summed, bf16[16,64,1848]{2,1,0:T(8,128)(2,1)} %a_in.3, bf16[928,512]{1,0:T(8,128)(2,1)} %copy-done.2, bf16[928,512]{1,0:T(8,128)(2,1)} %copy-done.8, bf16[928,512]{1,0:T(8,128)(2,1)} %copy-done.9, ...), custom_call_target="tpu_custom_call" | custom-call | flops 1000000 | bytes 1000000 | tf_op jit(solution)/shard_map/pallas_call | solution.py:49
  (70 shorter events, 28.3 us)
Async XLA Ops:
  8.0 9.1 %copy-start = (s32[16]{0:T(128)S(1)}, s32[16]{0:T(128)}, u32[]{:S(2)}) copy-start(s32[16]{0:T(128)} %param.13) | copy-start | bytes 196
  8.0 86.8 %all-gather.3.cloned.1.call-start = ((), (), s32[]{:S(2)}) async-start(), calls=%async_computation.2 | async-start | bytes 9437184 | tf_op jit(solution)/shard_map/all_gather | solution.py:320
  9.4 11.6 %copy-start.3 = (bf16[928,512]{1,0:T(8,128)(2,1)}, bf16[928,512]{1,0:T(8,128)(2,1)S(1)}, u32[]{:S(2)}) copy-start(bf16[928,512]{1,0:T(8,128)(2,1)S(1)} %slice.30.refs_0_) | copy-start | bytes 2850820
  9.4 27.6 %collective-permute-start.2 = (bf16[928,512]{1,0:T(8,128)(2,1)S(1)}, bf16[928,512]{1,0:T(8,128)(2,1)}, u32[]{:S(2)}, u32[]{:S(2)}) collective-permute-start(bf16[928,512]{1,0:T(8,128)(2,1)S(1)} %slice.30.refs_0_), channel_id=1, source_target_pairs={{4,0},{8,4},{12,8},{0,12},{5,1},{9,5},{13,9},{1,13},{6,2},{10,6},{... | collective-permute-start | bytes 2850824 | tf_op jit(solution)/shard_map/ppermute | solution.py:20
  12.3 24.7 %collective-permute-start.3 = (bf16[928,512]{1,0:T(8,128)(2,1)S(1)}, bf16[928,512]{1,0:T(8,128)(2,1)}, u32[]{:S(2)}, u32[]{:S(2)}) collective-permute-start(bf16[928,512]{1,0:T(8,128)(2,1)S(1)} %slice.30.refs_0_), channel_id=1, source_target_pairs={{12,0},{0,4},{4,8},{8,12},{13,1},{1,5},{5,9},{9,13},{14,2},{2,6},{... | collective-permute-start | bytes 2850824 | tf_op jit(solution)/shard_map/ppermute | solution.py:20
  13.4 23.6 %collective-permute-start = (bf16[512,512]{1,0:T(8,128)(2,1)}, bf16[512,512]{1,0:T(8,128)(2,1)S(1)}, u32[]{:S(2)}, u32[]{:S(2)}) collective-permute-start(bf16[512,512]{1,0:T(8,128)(2,1)} %get-tuple-element.46), channel_id=1, source_target_pairs={{0,0},{1,1},{2,16},{3,17},{16,2},{17,3},{18,18},{19,19},{4,4},{5,5... | collective-permute-start | bytes 1572872 | tf_op jit(solution)/shard_map/ppermute | solution.py:310
  15.1 21.9 %collective-permute-start.1 = (bf16[512,512]{1,0:T(8,128)(2,1)}, bf16[512,512]{1,0:T(8,128)(2,1)S(1)}, u32[]{:S(2)}, u32[]{:S(2)}) collective-permute-start(bf16[512,512]{1,0:T(8,128)(2,1)} %get-tuple-element.45), channel_id=1, source_target_pairs={{0,1},{1,0},{2,17},{3,16},{16,3},{17,2},{18,19},{19,18},{4,5},{5,4... | collective-permute-start | bytes 1572872 | tf_op jit(solution)/shard_map/ppermute | solution.py:310
  21.0 3.6 %collective-permute-start.4 = (bf16[128,512]{1,0:T(8,128)(2,1)S(1)}, bf16[128,512]{1,0:T(8,128)(2,1)S(1)}, u32[]{:S(2)}, u32[]{:S(2)}) collective-permute-start(bf16[128,512]{1,0:T(8,128)(2,1)S(1)} %shard_map.94), channel_id=1, source_target_pairs={{0,16},{16,0},{1,17},{17,1},{2,18},{18,2},{3,19},{19,3},{4,20},{20... | collective-permute-start | bytes 393224 | tf_op jit(solution)/shard_map/ppermute | solution.py:24
  24.7 5.8 %collective-permute-start.5 = (bf16[128,512]{1,0:T(8,128)(2,1)S(1)}, bf16[128,512]{1,0:T(8,128)(2,1)S(1)}, u32[]{:S(2)}, u32[]{:S(2)}) collective-permute-start(bf16[128,512]{1,0:T(8,128)(2,1)S(1)} %add.48), channel_id=1, source_target_pairs={{0,32},{32,0},{64,96},{96,64},{1,33},{33,1},{65,97},{97,65},{2,34}... | collective-permute-start | bytes 393224 | tf_op jit(solution)/shard_map/ppermute | solution.py:29
  30.6 6.4 %collective-permute-start.6 = (bf16[128,512]{1,0:T(8,128)(2,1)S(1)}, bf16[128,512]{1,0:T(8,128)(2,1)S(1)}, u32[]{:S(2)}, u32[]{:S(2)}) collective-permute-start(bf16[128,512]{1,0:T(8,128)(2,1)S(1)} %add.49), channel_id=1, source_target_pairs={{0,96},{96,0},{32,64},{64,32},{1,97},{97,1},{33,65},{65,33},{2,98}... | collective-permute-start | bytes 393224 | tf_op jit(solution)/shard_map/ppermute | solution.py:30
  38.1 77.5 %reduce-scatter.2.cloned.1.call-start = ((), (), s32[]{:S(2)}) async-start(), calls=%async_computation.1 | async-start | bytes 7536640 | tf_op jit(solution)/shard_map/reduce_scatter | solution.py:325
  48.3 22.3 %collective-permute-start.7 = (bf16[920,512]{1,0:T(8,128)(2,1)S(1)}, bf16[920,512]{1,0:T(8,128)(2,1)S(1)}, u32[]{:S(2)}, u32[]{:S(2)}) collective-permute-start(bf16[920,512]{1,0:T(8,128)(2,1)S(1)} %copy-done.4), channel_id=1, source_target_pairs={{4,0},{8,4},{12,8},{0,12},{5,1},{9,5},{13,9},{1,13},{6,2},{10,6},{... | collective-permute-start | bytes 2826248 | tf_op jit(solution)/shard_map/ppermute | solution.py:20
  51.6 22.6 %collective-permute-start.8 = (bf16[920,512]{1,0:T(8,128)(2,1)S(1)}, bf16[920,512]{1,0:T(8,128)(2,1)}, u32[]{:S(2)}, u32[]{:S(2)}) collective-permute-start(bf16[920,512]{1,0:T(8,128)(2,1)S(1)} %copy-done.4), channel_id=1, source_target_pairs={{12,0},{0,4},{4,8},{8,12},{13,1},{1,5},{5,9},{9,13},{14,2},{2,6},{... | collective-permute-start | bytes 2826248 | tf_op jit(solution)/shard_map/ppermute | solution.py:20
  74.1 20.7 %collective-permute-start.9 = (bf16[928,512]{1,0:T(8,128)(2,1)}, bf16[928,512]{1,0:T(8,128)(2,1)S(1)}, u32[]{:S(2)}, u32[]{:S(2)}) collective-permute-start(bf16[928,512]{1,0:T(8,128)(2,1)} %collective-permute-done.2.refs_1_), channel_id=1, source_target_pairs={{4,0},{8,4},{12,8},{0,12},{5,1},{9,5},{13,9},{1,13},{6,2},{10,6},{... | collective-permute-start | bytes 2850824 | tf_op jit(solution)/shard_map/ppermute | solution.py:20
  75.3 28.8 %collective-permute-start.13 = (bf16[920,512]{1,0:T(8,128)(2,1)}, bf16[920,512]{1,0:T(8,128)(2,1)S(1)}, u32[]{:S(2)}, u32[]{:S(2)}) collective-permute-start(bf16[920,512]{1,0:T(8,128)(2,1)} %collective-permute-done.8.refs_3_), channel_id=1, source_target_pairs={{12,0},{0,4},{4,8},{8,12},{13,1},{1,5},{5,9},{9,13},{14,2},{2,6},{... | collective-permute-start | bytes 2826248 | tf_op jit(solution)/shard_map/ppermute | solution.py:20
  103.0 26.2 %collective-permute-start.11 = (bf16[928,512]{1,0:T(8,128)(2,1)S(1)}, bf16[928,512]{1,0:T(8,128)(2,1)}, u32[]{:S(2)}, u32[]{:S(2)}) collective-permute-start(bf16[928,512]{1,0:T(8,128)(2,1)S(1)} %get-tuple-element.32), channel_id=1, source_target_pairs={{3,0},{0,1},{1,2},{2,3},{7,4},{4,5},{5,6},{6,7},{11,8},{8,9},{9,10... | collective-permute-start | bytes 2850824 | tf_op jit(solution)/shard_map/ppermute | solution.py:20
  113.3 25.2 %collective-permute-start.14 = (bf16[920,512]{1,0:T(8,128)(2,1)}, bf16[920,512]{1,0:T(8,128)(2,1)S(1)}, u32[]{:S(2)}, u32[]{:S(2)}) collective-permute-start(bf16[920,512]{1,0:T(8,128)(2,1)} %get-tuple-element.37), channel_id=1, source_target_pairs={{1,0},{2,1},{3,2},{0,3},{5,4},{6,5},{7,6},{4,7},{9,8},{10,9},{11,1... | collective-permute-start | bytes 2826248 | tf_op jit(solution)/shard_map/ppermute | solution.py:20
  117.0 24.7 %collective-permute-start.17 = (bf16[64,2944]{1,0:T(8,128)(2,1)S(1)}, bf16[64,2944]{1,0:T(8,128)(2,1)S(1)}, u32[]{:S(2)}, u32[]{:S(2)}) collective-permute-start(bf16[64,2944]{1,0:T(8,128)(2,1)S(1)} %get-tuple-element.43), channel_id=1, source_target_pairs={{12,0},{0,4},{4,8},{8,12},{13,1},{1,5},{5,9},{9,13},{14,2},{2,6},{... | collective-permute-start | bytes 1130504 | tf_op jit(solution)/shard_map/ppermute | solution.py:20
  118.8 54.9 %collective-permute-start.10 = (bf16[928,512]{1,0:T(8,128)(2,1)S(1)}, bf16[928,512]{1,0:T(8,128)(2,1)S(1)}, u32[]{:S(2)}, u32[]{:S(2)}) collective-permute-start(bf16[928,512]{1,0:T(8,128)(2,1)S(1)} %get-tuple-element.30), channel_id=1, source_target_pairs={{1,0},{2,1},{3,2},{0,3},{5,4},{6,5},{7,6},{4,7},{9,8},{10,9},{11,1... | collective-permute-start | bytes 2850824 | tf_op jit(solution)/shard_map/ppermute | solution.py:20
  130.6 43.1 %collective-permute-start.12 = (bf16[928,512]{1,0:T(8,128)(2,1)S(1)}, bf16[928,512]{1,0:T(8,128)(2,1)S(1)}, u32[]{:S(2)}, u32[]{:S(2)}) collective-permute-start(bf16[928,512]{1,0:T(8,128)(2,1)S(1)} %add.53), channel_id=1, source_target_pairs={{3,0},{0,1},{1,2},{2,3},{7,4},{4,5},{5,6},{6,7},{11,8},{8,9},{9,10... | collective-permute-start | bytes 2850824 | tf_op jit(solution)/shard_map/ppermute | solution.py:20
  130.7 43.0 %collective-permute-start.16 = (bf16[920,512]{1,0:T(8,128)(2,1)}, bf16[920,512]{1,0:T(8,128)(2,1)S(1)}, u32[]{:S(2)}, u32[]{:S(2)}) collective-permute-start(bf16[920,512]{1,0:T(8,128)(2,1)} %get-tuple-element.38), channel_id=1, source_target_pairs={{3,0},{0,1},{1,2},{2,3},{7,4},{4,5},{5,6},{6,7},{11,8},{8,9},{9,10... | collective-permute-start | bytes 2826248 | tf_op jit(solution)/shard_map/ppermute | solution.py:20
  138.8 35.0 %collective-permute-start.15 = (bf16[920,512]{1,0:T(8,128)(2,1)S(1)}, bf16[920,512]{1,0:T(8,128)(2,1)S(1)}, u32[]{:S(2)}, u32[]{:S(2)}) collective-permute-start(bf16[920,512]{1,0:T(8,128)(2,1)S(1)} %add.54), channel_id=1, source_target_pairs={{1,0},{2,1},{3,2},{0,3},{5,4},{6,5},{7,6},{4,7},{9,8},{10,9},{11,1... | collective-permute-start | bytes 2826248 | tf_op jit(solution)/shard_map/ppermute | solution.py:20
  141.7 10.3 %collective-permute-start.18 = (bf16[64,2944]{1,0:T(8,128)(2,1)S(1)}, bf16[64,2944]{1,0:T(8,128)(2,1)S(1)}, u32[]{:S(2)}, u32[]{:S(2)}) collective-permute-start(bf16[64,2944]{1,0:T(8,128)(2,1)S(1)} %get-tuple-element.42), channel_id=1, source_target_pairs={{8,0},{12,4},{0,8},{4,12},{9,1},{13,5},{1,9},{5,13},{10,2},{14,6},... | collective-permute-start | bytes 1130504 | tf_op jit(solution)/shard_map/ppermute | solution.py:20
  152.0 8.3 %collective-permute-start.19 = (bf16[64,2944]{1,0:T(8,128)(2,1)S(1)}, bf16[64,2944]{1,0:T(8,128)(2,1)S(1)}, u32[]{:S(2)}, u32[]{:S(2)}) collective-permute-start(bf16[64,2944]{1,0:T(8,128)(2,1)S(1)} %get-tuple-element.41), channel_id=1, source_target_pairs={{4,0},{8,4},{12,8},{0,12},{5,1},{9,5},{13,9},{1,13},{6,2},{10,6},{... | collective-permute-start | bytes 1130504 | tf_op jit(solution)/shard_map/ppermute | solution.py:20
  (10 other events, 24.6 us)
Sparse Core Ops, SparseCore 0:
  38.2 50.7 all-gather.2
Sparse Core Ops, SparseCore 1:
  47.2 66.8 reduce-scatter.1

commit v3 on v2

--- a/solution.py
+++ b/solution.py
@@ -257,39 +257,65 @@
     )
 
 
-def finish_kernel(slots, summed, a_in, *refs):
-    out = refs[-1]
-    rank = a_in.shape[1]
-    low = adapter_scale * lax.dot_general(
-        a_in[0], summed[:rank, :], TN, preferred_element_type=jnp.float32
-    )
-    start = 0
-    for k in range(0, len(refs) - 1, 3):
-        rows = refs[k].shape[0]
-        total = low[start : start + rows] + added(refs[k : k + 3], slice(None))
-        out[start : start + rows, :] = total.astype(out.dtype)
-        start += rows
-
-
-def finish(slots, summed, adapter_in, parts):
+def early_sums(slots, summed, adapter_in, parts):
     twice, tokens = summed.shape
     blocks = slots.shape[0]
     rows = tokens // blocks
     rank, units = adapter_in.shape[1:]
+    flat = [p for chunk in parts for p in chunk]
+
+    def kernel(slots, summed, a_in, *refs):
+        low = adapter_scale * lax.dot_general(
+            a_in[0], summed[:rank, :], TN, preferred_element_type=jnp.float32
+        )
+        start, at = 0, 0
+        for chunk, out in zip(parts, refs[len(flat) :]):
+            size = out.shape[0]
+            total = low[start : start + size] + added(refs[at : at + len(chunk)], slice(None))
+            out[...] = total.astype(out.dtype)
+            start, at = start + size, at + len(chunk)
+
+    shapes = [chunk[0].shape for chunk in parts]
+    block = lambda shape: pl.BlockSpec((shape[0], rows), lambda i, s: (0, i))
     return call(
-        finish_kernel,
+        kernel,
         (blocks,),
-        [slots, summed, adapter_in] + parts,
+        [slots, summed, adapter_in] + flat,
         [
             pl.BlockSpec((twice, rows), lambda i, s: (0, i)),
             pl.BlockSpec((1, rank, units), lambda i, s: (s[i], 0, 0)),
         ]
-        + [pl.BlockSpec((p.shape[0], rows), lambda i, s: (0, i)) for p in parts],
-        pl.BlockSpec((units, rows), lambda i, s: (0, i)),
-        jax.ShapeDtypeStruct((units, tokens), jnp.bfloat16),
+        + [block(p.shape) for p in flat],
+        [block(shape) for shape in shapes],
+        [jax.ShapeDtypeStruct(shape, jnp.bfloat16) for shape in shapes],
         [],
         BIG,
     )
+
+
+def finish(parts):
+    flat = [p for chunk in parts for p in chunk]
+    units = sum(chunk[0].shape[0] for chunk in parts)
+    tokens = flat[0].shape[1]
+    lanes = tokens // 2
+
+    def kernel(*refs):
+        start, at = 0, 0
+        for chunk in parts:
+            size = refs[at].shape[0]
+            total = added(refs[at : at + len(chunk)], slice(None))
+            refs[-1][start : start + size, :] = total.astype(refs[-1].dtype)
+            start, at = start + size, at + len(chunk)
+
+    return pl.pallas_call(
+        kernel,
+        grid=(tokens // lanes,),
+        in_specs=[pl.BlockSpec((p.shape[0], lanes), lambda i: (0, i)) for p in flat],
+        out_specs=pl.BlockSpec((units, lanes), lambda i: (0, i)),
+        out_shape=jax.ShapeDtypeStruct((units, tokens), jnp.bfloat16),
+        compiler_params=pltpu.CompilerParams(vmem_limit_bytes=20 * MIB),
+        cost_estimate=pl.CostEstimate(flops=1000000, bytes_accessed=1000000, transcendentals=0),
+    )(*flat)
 
 
 def body(hidden, cotangent, down_weight, adapter_in, adapter_out, adapter_ids, adapter_slot):
@@ -337,9 +363,12 @@
     left1, own1 = make(1, 3, 0)
     parts = scatter_ring(far0, right0, left0, own0, "z", 1)
     parts += scatter_ring(far1, right1, left1, own1, "z", -1)
-    hidden_gradient = finish(slots, summed, adapter_in, parts)
-
-    grad_in, grad_out = last_sum(second_hop(sums, "x"), units, cotangent.shape[1])
+    own0, left0, right0, own1, left1, right1 = parts
+    ready = early_sums(slots, summed, adapter_in, [[own0, left0], [own1]])
+    sums = second_hop(sums, "x")
+    *ready, sums[0] = barrier((*ready, sums[0]))
+    hidden_gradient = finish([[ready[0], right0], [ready[1], left1, right1]])
+    grad_in, grad_out = last_sum(sums, units, cotangent.shape[1])
     return hidden_gradient.T, grad_in, grad_out
 
 

time: 189 us -> 182 us (0.963)
  waiting for transfers between devices: 73.5 us -> 61.6 us
  starting transfers between devices: 35.3 us -> 39.1 us
  local copies, waits for them, and re-layouts: 12.3 us -> 9.92 us
  Pallas kernels: 49.5 us -> 51.6 us
    ppermute x15, waiting for transfers between devices: 67.2 us -> 55.3 us  [take_from(): return lax.ppermute(array, axis, [((i + step) % N, i) for i in range(N)])]
    ppermute x15, starting transfers between devices: 24.2 us -> 27.9 us  [take_from(): return lax.ppermute(array, axis, [((i + step) % N, i) for i in range(N)])]
    unnamed x24 -> x22, local copies, waits for them, and re-layouts: 5.62 us -> 3.18 us
  transfers between devices with their start and end apart: 22 -> 22, of which waited for: 10 -> 9; matrix products, arithmetic and copies ran while one was open for 4% -> 4% of each run, Pallas kernels for 23% -> 27%
where the time goes in v3:
time: 182 us; the launch traced here: 181 us
  waiting for transfers between devices  61.6 us (34%)
  Pallas kernels  51.6 us (28%)
  starting transfers between devices  39.1 us (21%)
  between operations  15.7 us (9%)
  local copies, waits for them, and re-layouts  9.92 us (5%)
  other arithmetic  2.73 us (2%)
    ppermute x15, waiting for transfers between devices, take_from(): return lax.ppermute(array, axis, [((i + step) % N, i) for i in range(N)])  55.3 us
    pallas_call x7, Pallas kernels, call(): pl.pallas_call(kernel, grid_spec=pltpu.PrefetchScalarGridSpec(num_scalar_...  47.8 us
    ppermute x15, starting transfers between devices, take_from(): return lax.ppermute(array, axis, [((i + step) % N, i) for i in range(N)])  27.9 us
    slice x2, local copies, waits for them, and re-layouts, body(): own = [down_weight[:first], down_weight[first:]]  4.49 us
    ppermute x1, waiting for transfers between devices, sum_over_dp(): array = array + lax.ppermute(array, 'y', [(0, 1), (1, 0), (2, 3), (3, 2)])  4.17 us
  transfers between devices with their start and end apart: 22, of which 9 were waited for; matrix products, arithmetic and copies ran while one was open for 4% of the time, Pallas kernels for 27%

profile of v3, /device:TPU:0, one launch (start us, length us, event | category | flops | bytes accessed | tf_op | source)
XLA Modules:
  0.0 180.6 jit_solution(2001036042379781909)
XLA Ops:
  8.1 2.3 %slice.30.refs_0_ = bf16[928,512]{1,0:T(8,128)(2,1)} slice(bf16[1848,512]{1,0:T(8,128)(2,1)} %param.9), slice={[0:928], [0:512]} | slice | bytes 1900544 | tf_op jit(solution)/shard_map/slice | solution.py:338
  17.2 3.3 %shard_map.94 = bf16[128,512]{1,0:T(8,128)(2,1)S(1)} custom-call(s32[4]{0:T(128)S(1)} %gather_fusion, bf16[512,1024]{1,0:T(8,128)(2,1)S(1)} %copy-done.1, bf16[1848,512]{1,0:T(8,128)(2,1)} %bitcast.22, bf16[16,64,1024]{2,1,0:T(8,128)(2,1)} %a_out.1, bf16[16,64,1848]{2,1,0:T(8,128)(2,1)} %a_in.3), custom_call_target="tpu_custom_call" | custom-call | flops 1000000 | bytes 1000000 | tf_op jit(solution)/shard_map/pallas_call | solution.py:49
  20.5 3.5 %collective-permute-start.4 = (bf16[128,512]{1,0:T(8,128)(2,1)S(1)}, bf16[128,512]{1,0:T(8,128)(2,1)S(1)}, u32[]{:S(2)}, u32[]{:S(2)}) collective-permute-start(bf16[128,512]{1,0:T(8,128)(2,1)S(1)} %shard_map.94), channel_id=1, source_target_pairs={{0,16},{16,0},{1,17},{17,1},{2,18},{18,2},{3,19},{19,3},{4,20},{20... | collective-permute-start | bytes 393224 | tf_op jit(solution)/shard_map/ppermute | solution.py:24
  26.7 4.2 %collective-permute-done.5 = bf16[128,512]{1,0:T(8,128)(2,1)S(1)} collective-permute-done((bf16[128,512]{1,0:T(8,128)(2,1)S(1)}, bf16[128,512]{1,0:T(8,128)(2,1)S(1)}, u32[]{:S(2)}, u32[]{:S(2)}) %collective-permute-start.5) | collective-permute-done | bytes 131104 | tf_op jit(solution)/shard_map/ppermute | solution.py:29
  30.9 3.1 %collective-permute-start.6 = (bf16[128,512]{1,0:T(8,128)(2,1)S(1)}, bf16[128,512]{1,0:T(8,128)(2,1)S(1)}, u32[]{:S(2)}, u32[]{:S(2)}) collective-permute-start(bf16[128,512]{1,0:T(8,128)(2,1)S(1)} %add.49), channel_id=1, source_target_pairs={{0,96},{96,0},{32,64},{64,32},{1,97},{97,1},{33,65},{65,33},{2,98}... | collective-permute-start | bytes 393224 | tf_op jit(solution)/shard_map/ppermute | solution.py:30
  38.6 8.8 %shard_map.96 = bf16[4,256,2944]{2,1,0:T(8,128)(2,1)} custom-call(s32[5]{0:T(128)S(1)} %pad_add_fusion.index, bf16[128,512]{1,0:T(8,128)(2,1)S(1)} %add.50.summed, bf16[512,1024]{1,0:T(8,128)(2,1)S(1)} %copy-done.1, bf16[1848,512]{1,0:T(8,128)(2,1)} %bitcast.23), custom_call_target="tpu_custom_call" | custom-call | flops 1000000 | bytes 1000000 | tf_op jit(solution)/shard_map/pallas_call | solution.py:49
  49.0 3.0 %collective-permute-start.7 = (bf16[920,512]{1,0:T(8,128)(2,1)S(1)}, bf16[920,512]{1,0:T(8,128)(2,1)S(1)}, u32[]{:S(2)}, u32[]{:S(2)}) collective-permute-start(bf16[920,512]{1,0:T(8,128)(2,1)S(1)} %copy-done.6), channel_id=1, source_target_pairs={{4,0},{8,4},{12,8},{0,12},{5,1},{9,5},{13,9},{1,13},{6,2},{10,6},{... | collective-permute-start | bytes 2826248 | tf_op jit(solution)/shard_map/ppermute | solution.py:20
  52.0 19.6 %collective-permute-done.8.refs_3_ = bf16[920,512]{1,0:T(8,128)(2,1)S(1)} collective-permute-done((bf16[920,512]{1,0:T(8,128)(2,1)S(1)}, bf16[920,512]{1,0:T(8,128)(2,1)S(1)}, u32[]{:S(2)}, u32[]{:S(2)}) %collective-permute-start.8) | collective-permute-done | bytes 942112 | tf_op jit(solution)/shard_map/ppermute | solution.py:20
  71.5 3.0 %collective-permute-start.9 = (bf16[928,512]{1,0:T(8,128)(2,1)}, bf16[928,512]{1,0:T(8,128)(2,1)S(1)}, u32[]{:S(2)}, u32[]{:S(2)}) collective-permute-start(bf16[928,512]{1,0:T(8,128)(2,1)} %collective-permute-done.2.refs_1_), channel_id=1, source_target_pairs={{4,0},{8,4},{12,8},{0,12},{5,1},{9,5},{13,9},{1,13},{6,2},{10,6},{... | collective-permute-start | bytes 2850824 | tf_op jit(solution)/shard_map/ppermute | solution.py:20
  74.6 18.4 %collective-permute-done.9.refs_2_ = bf16[928,512]{1,0:T(8,128)(2,1)S(1)} collective-permute-done((bf16[928,512]{1,0:T(8,128)(2,1)}, bf16[928,512]{1,0:T(8,128)(2,1)S(1)}, u32[]{:S(2)}, u32[]{:S(2)}) %collective-permute-start.9) | collective-permute-done | bytes 950304 | tf_op jit(solution)/shard_map/ppermute | solution.py:20
  93.9 8.1 %shard_map.98 = (bf16[928,512]{1,0:T(8,128)(2,1)S(1)}, bf16[928,512]{1,0:T(8,128)(2,1)}) custom-call(s32[3]{0:T(128)S(1)} %get-tuple-element.58.index, bf16[4,2,2,512,512]{4,3,2,1,0:T(8,128)(2,1)} %bitcast.18, bf16[928,512]{1,0:T(8,128)(2,1)} %slice.30.refs_0_, bf16[928,512]{1,0:T(8,128)(2,1)} %collective-permute-done.2.refs_1_, bf16[928,512]{1,0:T(8,128)(2,1)} %copy-done.7, ...), custom_call_target="tpu_custom_call" | custom-call | flops 1000000 | bytes 1000000 | tf_op jit(solution)/shard_map/pallas_call | solution.py:49
  103.0 8.1 %shard_map.101 = (bf16[920,512]{1,0:T(8,128)(2,1)S(1)}, bf16[920,512]{1,0:T(8,128)(2,1)}) custom-call(s32[3]{0:T(128)S(1)} %get-tuple-element.60.index, bf16[4,2,2,512,512]{4,3,2,1,0:T(8,128)(2,1)} %bitcast.19, bf16[920,512]{1,0:T(8,128)(2,1)} %slice.31.refs_0_, bf16[920,512]{1,0:T(8,128)(2,1)} %copy-done.9, ...), custom_call_target="tpu_custom_call" | custom-call | flops 1000000 | bytes 1000000 | tf_op jit(solution)/shard_map/pallas_call | solution.py:49
  111.1 2.6 %collective-permute-start.14 = (bf16[920,512]{1,0:T(8,128)(2,1)S(1)}, bf16[920,512]{1,0:T(8,128)(2,1)S(1)}, u32[]{:S(2)}, u32[]{:S(2)}) collective-permute-start(bf16[920,512]{1,0:T(8,128)(2,1)S(1)} %get-tuple-element.46), channel_id=1, source_target_pairs={{1,0},{2,1},{3,2},{0,3},{5,4},{6,5},{7,6},{4,7},{9,8},{10,9},{11,1... | collective-permute-start | bytes 2826248 | tf_op jit(solution)/shard_map/ppermute | solution.py:20
  113.8 3.2 %collective-permute-start.10 = (bf16[928,512]{1,0:T(8,128)(2,1)}, bf16[928,512]{1,0:T(8,128)(2,1)}, u32[]{:S(2)}, u32[]{:S(2)}) collective-permute-start(bf16[928,512]{1,0:T(8,128)(2,1)} %get-tuple-element.35), channel_id=1, source_target_pairs={{1,0},{2,1},{3,2},{0,3},{5,4},{6,5},{7,6},{4,7},{9,8},{10,9},{11,1... | collective-permute-start | bytes 2850824 | tf_op jit(solution)/shard_map/ppermute | solution.py:20
  117.0 7.2 %shard_map.99 = (bf16[920,512]{1,0:T(8,128)(2,1)S(1)}, bf16[920,512]{1,0:T(8,128)(2,1)S(1)}) custom-call(s32[3]{0:T(128)S(1)} %get-tuple-element.59.index, bf16[4,2,2,512,512]{4,3,2,1,0:T(8,128)(2,1)} %bitcast.20, bf16[920,512]{1,0:T(8,128)(2,1)} %slice.31.refs_0_, bf16[920,512]{1,0:T(8,128)(2,1)} %copy-done.9, ...), custom_call_target="tpu_custom_call" | custom-call | flops 1000000 | bytes 1000000 | tf_op jit(solution)/shard_map/pallas_call | solution.py:49
  125.2 7.2 %shard_map.97 = (bf16[928,512]{1,0:T(8,128)(2,1)S(1)}, bf16[928,512]{1,0:T(8,128)(2,1)S(1)}) custom-call(s32[3]{0:T(128)S(1)} %get-tuple-element.57.index, bf16[4,2,2,512,512]{4,3,2,1,0:T(8,128)(2,1)} %bitcast.21, bf16[928,512]{1,0:T(8,128)(2,1)} %slice.30.refs_0_, bf16[928,512]{1,0:T(8,128)(2,1)} %collective-permute-done.2.refs_1_, ...), custom_call_target="tpu_custom_call" | custom-call | flops 1000000 | bytes 1000000 | tf_op jit(solution)/shard_map/pallas_call | solution.py:49
  132.4 2.7 %collective-permute-done.14 = bf16[920,512]{1,0:T(8,128)(2,1)S(1)} collective-permute-done((bf16[920,512]{1,0:T(8,128)(2,1)S(1)}, bf16[920,512]{1,0:T(8,128)(2,1)S(1)}, u32[]{:S(2)}, u32[]{:S(2)}) %collective-permute-start.14) | collective-permute-done | bytes 942112 | tf_op jit(solution)/shard_map/ppermute | solution.py:20
  136.3 3.7 %collective-permute-start.15 = (bf16[920,512]{1,0:T(8,128)(2,1)}, bf16[920,512]{1,0:T(8,128)(2,1)S(1)}, u32[]{:S(2)}, u32[]{:S(2)}) collective-permute-start(bf16[920,512]{1,0:T(8,128)(2,1)} %add.54), channel_id=1, source_target_pairs={{1,0},{2,1},{3,2},{0,3},{5,4},{6,5},{7,6},{4,7},{9,8},{10,9},{11,1... | collective-permute-start | bytes 2826248 | tf_op jit(solution)/shard_map/ppermute | solution.py:20
  142.7 3.6 %collective-permute-start.19 = (bf16[64,2944]{1,0:T(8,128)(2,1)S(1)}, bf16[64,2944]{1,0:T(8,128)(2,1)S(1)}, u32[]{:S(2)}, u32[]{:S(2)}) collective-permute-start(bf16[64,2944]{1,0:T(8,128)(2,1)S(1)} %get-tuple-element.51), channel_id=1, source_target_pairs={{4,0},{8,4},{12,8},{0,12},{5,1},{9,5},{13,9},{1,13},{6,2},{10,6},{... | collective-permute-start | bytes 1130504 | tf_op jit(solution)/shard_map/ppermute | solution.py:20
  146.3 8.3 %collective-permute-done.19.after = bf16[64,2944]{1,0:T(8,128)(2,1)S(1)} collective-permute-done((bf16[64,2944]{1,0:T(8,128)(2,1)S(1)}, bf16[64,2944]{1,0:T(8,128)(2,1)S(1)}, u32[]{:S(2)}, u32[]{:S(2)}) %collective-permute-start.19) | collective-permute-done | bytes 376864 | tf_op jit(solution)/shard_map/ppermute | solution.py:20
  155.7 3.5 %collective-permute-start.17 = (bf16[64,2944]{1,0:T(8,128)(2,1)S(1)}, bf16[64,2944]{1,0:T(8,128)(2,1)S(1)}, u32[]{:S(2)}, u32[]{:S(2)}) collective-permute-start(bf16[64,2944]{1,0:T(8,128)(2,1)S(1)} %get-tuple-element.53), channel_id=1, source_target_pairs={{12,0},{0,4},{4,8},{8,12},{13,1},{1,5},{5,9},{9,13},{14,2},{2,6},{... | collective-permute-start | bytes 1130504 | tf_op jit(solution)/shard_map/ppermute | solution.py:20
  159.2 5.0 %shard_map.100 = (bf16[928,512]{1,0:T(8,128)(2,1)}, bf16[920,512]{1,0:T(8,128)(2,1)S(1)}) custom-call(s32[4]{0:T(128)S(1)} %gather_fusion, bf16[128,512]{1,0:T(8,128)(2,1)S(1)} %add.50.summed, bf16[16,64,1848]{2,1,0:T(8,128)(2,1)} %a_in.3, bf16[928,512]{1,0:T(8,128)(2,1)} %copy-done.3, bf16[928,512]{1,0:T(8,128)(2,1)} %collective-permute-done.10.refs_1_, ...), custom_call_target="tpu_custom_call" | custom-call | flops 1000000 | bytes 1000000 | tf_op jit(solution)/shard_map/pallas_call | solution.py:49
  164.2 3.6 %collective-permute-done.17.across = bf16[64,2944]{1,0:T(8,128)(2,1)S(1)} collective-permute-done((bf16[64,2944]{1,0:T(8,128)(2,1)S(1)}, bf16[64,2944]{1,0:T(8,128)(2,1)S(1)}, u32[]{:S(2)}, u32[]{:S(2)}) %collective-permute-start.17) | collective-permute-done | bytes 376864 | tf_op jit(solution)/shard_map/ppermute | solution.py:20
  168.7 2.6 %collective-permute-done.15.refs_3_ = bf16[920,512]{1,0:T(8,128)(2,1)S(1)} collective-permute-done((bf16[920,512]{1,0:T(8,128)(2,1)}, bf16[920,512]{1,0:T(8,128)(2,1)S(1)}, u32[]{:S(2)}, u32[]{:S(2)}) %collective-permute-start.15) | collective-permute-done | bytes 942112 | tf_op jit(solution)/shard_map/ppermute | solution.py:20
  (69 shorter events, 26.2 us)
Async XLA Ops:
  8.0 84.9 %all-gather.3.cloned.1.call-start = ((), (), s32[]{:S(2)}) async-start(), calls=%async_computation.2 | async-start | bytes 9437184 | tf_op jit(solution)/shard_map/all_gather | solution.py:346
  10.4 27.1 %collective-permute-start.3 = (bf16[928,512]{1,0:T(8,128)(2,1)}, bf16[928,512]{1,0:T(8,128)(2,1)}, u32[]{:S(2)}, u32[]{:S(2)}) collective-permute-start(bf16[928,512]{1,0:T(8,128)(2,1)} %slice.30.refs_0_), channel_id=1, source_target_pairs={{12,0},{0,4},{4,8},{8,12},{13,1},{1,5},{5,9},{9,13},{14,2},{2,6},{... | collective-permute-start | bytes 2850824 | tf_op jit(solution)/shard_map/ppermute | solution.py:20
  11.9 25.5 %collective-permute-start.2 = (bf16[928,512]{1,0:T(8,128)(2,1)}, bf16[928,512]{1,0:T(8,128)(2,1)}, u32[]{:S(2)}, u32[]{:S(2)}) collective-permute-start(bf16[928,512]{1,0:T(8,128)(2,1)} %slice.30.refs_0_), channel_id=1, source_target_pairs={{4,0},{8,4},{12,8},{0,12},{5,1},{9,5},{13,9},{1,13},{6,2},{10,6},{... | collective-permute-start | bytes 2850824 | tf_op jit(solution)/shard_map/ppermute | solution.py:20
  13.7 23.7 %collective-permute-start.1 = (bf16[512,512]{1,0:T(8,128)(2,1)S(1)}, bf16[512,512]{1,0:T(8,128)(2,1)S(1)}, u32[]{:S(2)}, u32[]{:S(2)}) collective-permute-start(bf16[512,512]{1,0:T(8,128)(2,1)S(1)} %get-tuple-element.55), channel_id=1, source_target_pairs={{0,1},{1,0},{2,17},{3,16},{16,3},{17,2},{18,19},{19,18},{4,5},{5,4... | collective-permute-start | bytes 1572872 | tf_op jit(solution)/shard_map/ppermute | solution.py:336
  15.8 21.6 %collective-permute-start = (bf16[512,512]{1,0:T(8,128)(2,1)S(1)}, bf16[512,512]{1,0:T(8,128)(2,1)S(1)}, u32[]{:S(2)}, u32[]{:S(2)}) collective-permute-start(bf16[512,512]{1,0:T(8,128)(2,1)S(1)} %get-tuple-element.56), channel_id=1, source_target_pairs={{0,0},{1,1},{2,16},{3,17},{16,2},{17,3},{18,18},{19,19},{4,4},{5,5... | collective-permute-start | bytes 1572872 | tf_op jit(solution)/shard_map/ppermute | solution.py:336
  20.5 4.5 %collective-permute-start.4 = (bf16[128,512]{1,0:T(8,128)(2,1)S(1)}, bf16[128,512]{1,0:T(8,128)(2,1)S(1)}, u32[]{:S(2)}, u32[]{:S(2)}) collective-permute-start(bf16[128,512]{1,0:T(8,128)(2,1)S(1)} %shard_map.94), channel_id=1, source_target_pairs={{0,16},{16,0},{1,17},{17,1},{2,18},{18,2},{3,19},{19,3},{4,20},{20... | collective-permute-start | bytes 393224 | tf_op jit(solution)/shard_map/ppermute | solution.py:24
  25.1 5.8 %collective-permute-start.5 = (bf16[128,512]{1,0:T(8,128)(2,1)S(1)}, bf16[128,512]{1,0:T(8,128)(2,1)S(1)}, u32[]{:S(2)}, u32[]{:S(2)}) collective-permute-start(bf16[128,512]{1,0:T(8,128)(2,1)S(1)} %add.48), channel_id=1, source_target_pairs={{0,32},{32,0},{64,96},{96,64},{1,33},{33,1},{65,97},{97,65},{2,34}... | collective-permute-start | bytes 393224 | tf_op jit(solution)/shard_map/ppermute | solution.py:29
  30.9 6.4 %collective-permute-start.6 = (bf16[128,512]{1,0:T(8,128)(2,1)S(1)}, bf16[128,512]{1,0:T(8,128)(2,1)S(1)}, u32[]{:S(2)}, u32[]{:S(2)}) collective-permute-start(bf16[128,512]{1,0:T(8,128)(2,1)S(1)} %add.49), channel_id=1, source_target_pairs={{0,96},{96,0},{32,64},{64,32},{1,97},{97,1},{33,65},{65,33},{2,98}... | collective-permute-start | bytes 393224 | tf_op jit(solution)/shard_map/ppermute | solution.py:30
  38.5 102.7 %reduce-scatter.2.cloned.1.call-start = ((), (), s32[]{:S(2)}) async-start(), calls=%async_computation.1 | async-start | bytes 7536640 | tf_op jit(solution)/shard_map/reduce_scatter | solution.py:351
  48.7 22.8 %collective-permute-start.8 = (bf16[920,512]{1,0:T(8,128)(2,1)S(1)}, bf16[920,512]{1,0:T(8,128)(2,1)S(1)}, u32[]{:S(2)}, u32[]{:S(2)}) collective-permute-start(bf16[920,512]{1,0:T(8,128)(2,1)S(1)} %copy-done.6), channel_id=1, source_target_pairs={{12,0},{0,4},{4,8},{8,12},{13,1},{1,5},{5,9},{9,13},{14,2},{2,6},{... | collective-permute-start | bytes 2826248 | tf_op jit(solution)/shard_map/ppermute | solution.py:20
  49.0 22.6 %collective-permute-start.7 = (bf16[920,512]{1,0:T(8,128)(2,1)S(1)}, bf16[920,512]{1,0:T(8,128)(2,1)S(1)}, u32[]{:S(2)}, u32[]{:S(2)}) collective-permute-start(bf16[920,512]{1,0:T(8,128)(2,1)S(1)} %copy-done.6), channel_id=1, source_target_pairs={{4,0},{8,4},{12,8},{0,12},{5,1},{9,5},{13,9},{1,13},{6,2},{10,6},{... | collective-permute-start | bytes 2826248 | tf_op jit(solution)/shard_map/ppermute | solution.py:20
  71.5 30.5 %copy-start.8 = (bf16[920,512]{1,0:T(8,128)(2,1)}, bf16[920,512]{1,0:T(8,128)(2,1)S(1)}, u32[]{:S(2)}) copy-start(bf16[920,512]{1,0:T(8,128)(2,1)S(1)} %collective-permute-done.8.refs_3_) | copy-start | bytes 2826244
  71.5 30.6 %copy-start.9 = (bf16[920,512]{1,0:T(8,128)(2,1)}, bf16[920,512]{1,0:T(8,128)(2,1)S(1)}, u32[]{:S(2)}) copy-start(bf16[920,512]{1,0:T(8,128)(2,1)S(1)} %collective-permute-done.7.refs_1_) | copy-start | bytes 2826244
  71.5 21.4 %collective-permute-start.9 = (bf16[928,512]{1,0:T(8,128)(2,1)}, bf16[928,512]{1,0:T(8,128)(2,1)S(1)}, u32[]{:S(2)}, u32[]{:S(2)}) collective-permute-start(bf16[928,512]{1,0:T(8,128)(2,1)} %collective-permute-done.2.refs_1_), channel_id=1, source_target_pairs={{4,0},{8,4},{12,8},{0,12},{5,1},{9,5},{13,9},{1,13},{6,2},{10,6},{... | collective-permute-start | bytes 2850824 | tf_op jit(solution)/shard_map/ppermute | solution.py:20
  74.5 28.5 %collective-permute-start.11 = (bf16[920,512]{1,0:T(8,128)(2,1)S(1)}, bf16[920,512]{1,0:T(8,128)(2,1)}, u32[]{:S(2)}, u32[]{:S(2)}) collective-permute-start(bf16[920,512]{1,0:T(8,128)(2,1)S(1)} %collective-permute-done.8.refs_3_), channel_id=1, source_target_pairs={{12,0},{0,4},{4,8},{8,12},{13,1},{1,5},{5,9},{9,13},{14,2},{2,6},{... | collective-permute-start | bytes 2826248 | tf_op jit(solution)/shard_map/ppermute | solution.py:20
  102.1 37.9 %collective-permute-start.12 = (bf16[928,512]{1,0:T(8,128)(2,1)S(1)}, bf16[928,512]{1,0:T(8,128)(2,1)S(1)}, u32[]{:S(2)}, u32[]{:S(2)}) collective-permute-start(bf16[928,512]{1,0:T(8,128)(2,1)S(1)} %get-tuple-element.43), channel_id=1, source_target_pairs={{3,0},{0,1},{1,2},{2,3},{7,4},{4,5},{5,6},{6,7},{11,8},{8,9},{9,10... | collective-permute-start | bytes 2850824 | tf_op jit(solution)/shard_map/ppermute | solution.py:20
  111.1 24.0 %collective-permute-start.14 = (bf16[920,512]{1,0:T(8,128)(2,1)S(1)}, bf16[920,512]{1,0:T(8,128)(2,1)S(1)}, u32[]{:S(2)}, u32[]{:S(2)}) collective-permute-start(bf16[920,512]{1,0:T(8,128)(2,1)S(1)} %get-tuple-element.46), channel_id=1, source_target_pairs={{1,0},{2,1},{3,2},{0,3},{5,4},{6,5},{7,6},{4,7},{9,8},{10,9},{11,1... | collective-permute-start | bytes 2826248 | tf_op jit(solution)/shard_map/ppermute | solution.py:20
  113.8 54.9 %collective-permute-start.16 = (bf16[920,512]{1,0:T(8,128)(2,1)}, bf16[920,512]{1,0:T(8,128)(2,1)S(1)}, u32[]{:S(2)}, u32[]{:S(2)}) collective-permute-start(bf16[920,512]{1,0:T(8,128)(2,1)} %get-tuple-element.47), channel_id=1, source_target_pairs={{3,0},{0,1},{1,2},{2,3},{7,4},{4,5},{5,6},{6,7},{11,8},{8,9},{9,10... | collective-permute-start | bytes 2826248 | tf_op jit(solution)/shard_map/ppermute | solution.py:20
  113.8 41.9 %collective-permute-start.10 = (bf16[928,512]{1,0:T(8,128)(2,1)}, bf16[928,512]{1,0:T(8,128)(2,1)}, u32[]{:S(2)}, u32[]{:S(2)}) collective-permute-start(bf16[928,512]{1,0:T(8,128)(2,1)} %get-tuple-element.35), channel_id=1, source_target_pairs={{1,0},{2,1},{3,2},{0,3},{5,4},{6,5},{7,6},{4,7},{9,8},{10,9},{11,1... | collective-permute-start | bytes 2850824 | tf_op jit(solution)/shard_map/ppermute | solution.py:20
  136.3 35.0 %collective-permute-start.15 = (bf16[920,512]{1,0:T(8,128)(2,1)}, bf16[920,512]{1,0:T(8,128)(2,1)S(1)}, u32[]{:S(2)}, u32[]{:S(2)}) collective-permute-start(bf16[920,512]{1,0:T(8,128)(2,1)} %add.54), channel_id=1, source_target_pairs={{1,0},{2,1},{3,2},{0,3},{5,4},{6,5},{7,6},{4,7},{9,8},{10,9},{11,1... | collective-permute-start | bytes 2826248 | tf_op jit(solution)/shard_map/ppermute | solution.py:20
  141.2 30.1 %collective-permute-start.13 = (bf16[928,512]{1,0:T(8,128)(2,1)}, bf16[928,512]{1,0:T(8,128)(2,1)S(1)}, u32[]{:S(2)}, u32[]{:S(2)}) collective-permute-start(bf16[928,512]{1,0:T(8,128)(2,1)} %add.53), channel_id=1, source_target_pairs={{3,0},{0,1},{1,2},{2,3},{7,4},{4,5},{5,6},{6,7},{11,8},{8,9},{9,10... | collective-permute-start | bytes 2850824 | tf_op jit(solution)/shard_map/ppermute | solution.py:20
  142.7 11.9 %collective-permute-start.19 = (bf16[64,2944]{1,0:T(8,128)(2,1)S(1)}, bf16[64,2944]{1,0:T(8,128)(2,1)S(1)}, u32[]{:S(2)}, u32[]{:S(2)}) collective-permute-start(bf16[64,2944]{1,0:T(8,128)(2,1)S(1)} %get-tuple-element.51), channel_id=1, source_target_pairs={{4,0},{8,4},{12,8},{0,12},{5,1},{9,5},{13,9},{1,13},{6,2},{10,6},{... | collective-permute-start | bytes 1130504 | tf_op jit(solution)/shard_map/ppermute | solution.py:20
  154.6 9.6 %collective-permute-start.18 = (bf16[64,2944]{1,0:T(8,128)(2,1)S(1)}, bf16[64,2944]{1,0:T(8,128)(2,1)S(1)}, u32[]{:S(2)}, u32[]{:S(2)}) collective-permute-start(bf16[64,2944]{1,0:T(8,128)(2,1)S(1)} %get-tuple-element.52), channel_id=1, source_target_pairs={{8,0},{12,4},{0,8},{4,12},{9,1},{13,5},{1,9},{5,13},{10,2},{14,6},... | collective-permute-start | bytes 1130504 | tf_op jit(solution)/shard_map/ppermute | solution.py:20
  155.7 12.1 %collective-permute-start.17 = (bf16[64,2944]{1,0:T(8,128)(2,1)S(1)}, bf16[64,2944]{1,0:T(8,128)(2,1)S(1)}, u32[]{:S(2)}, u32[]{:S(2)}) collective-permute-start(bf16[64,2944]{1,0:T(8,128)(2,1)S(1)} %get-tuple-element.53), channel_id=1, source_target_pairs={{12,0},{0,4},{4,8},{8,12},{13,1},{1,5},{5,9},{9,13},{14,2},{2,6},{... | collective-permute-start | bytes 1130504 | tf_op jit(solution)/shard_map/ppermute | solution.py:20
  (9 other events, 58.4 us)
Sparse Core Ops, SparseCore 0:
  38.6 49.7 all-gather.2
Sparse Core Ops, SparseCore 1:
  47.6 65.9 reduce-scatter.1

commit v4 on v3

--- a/solution.py
+++ b/solution.py
@@ -119,7 +119,7 @@
     wide = width + units
     wide = wide + -wide % 128
     rank = summed.shape[0] // 2
-    shape = (N, N * rank, wide)
+    shape = (N, N, rank, wide)
 
     def kernel(index, summed, cotangent, hidden, out, products, staged, sems):
         for b in range(blocks):
@@ -132,15 +132,17 @@
             )
             products[b, :, width + units :] = jnp.zeros((rank, wide - width - units), jnp.float32)
         x = index[blocks]
+        staged[...] = jnp.zeros(staged.shape, staged.dtype)
+        for b in range(blocks):
+            total = jnp.float32(multiplier) * products[b]
+            for other in range(blocks):
+                if other != b:
+                    same = jnp.where(index[other] == index[b], multiplier, 0.0)
+                    total = total + same.astype(jnp.float32) * products[other]
+            place = lax.rem(lax.div(index[b], N) - x + N, N)
+            staged[lax.rem(index[b], N), place] = total.astype(staged.dtype)
         copies = []
         for s in range(N):
-            for t in range(N):
-                slot = lax.rem(x + t, N) * N + s
-                total = jnp.zeros((rank, wide), jnp.float32)
-                for b in range(blocks):
-                    weight = jnp.where(index[b] == slot, jnp.float32(multiplier), jnp.float32(0))
-                    total = total + weight * products[b]
-                staged[s, t * rank : (t + 1) * rank, :] = total.astype(staged.dtype)
             copies.append(pltpu.make_async_copy(staged.at[s], out.at[s], sems.at[s]))
             copies[s].start()
         for copy in copies:
@@ -348,6 +350,7 @@
     before.append(take_from(own[1], "x", -1))
     index = jnp.concatenate([slots, x[None].astype(jnp.int32)])
     terms = gradient_terms(index, summed, cotangent, hidden, adapter_scale / math.sqrt(tokens))
+    terms = terms.reshape(N, -1, terms.shape[3])
     sums = lax.psum_scatter(terms, "z", scatter_dimension=0)
     after[0], after[1], before[1], terms = barrier((after[0], after[1], before[1], terms))
     fars = [take_from(after[0], "x", 1), take_from(before[1], "x", -1)]

time: 182 us -> 180 us (0.989)
  Pallas kernels: 51.6 us -> 49.3 us
    pallas_call x7, Pallas kernels: 47.8 us -> 45.6 us  [call(): pl.pallas_call(kernel, grid_spec=pltpu.PrefetchScalarGridSpec(num_scalar_...]
  transfers between devices with their start and end apart: 22 -> 22, of which waited for: 9 -> 9; matrix products, arithmetic and copies ran while one was open for 4% -> 4% of each run, Pallas kernels for 27% -> 26%
where the time goes in v4:
time: 180 us; the launch traced here: 179 us
  waiting for transfers between devices  62.6 us (35%)
  Pallas kernels  49.3 us (27%)
  starting transfers between devices  39.2 us (22%)
  between operations  15.7 us (9%)
  local copies, waits for them, and re-layouts  9.84 us (5%)
  other arithmetic  2.74 us (2%)
    ppermute x15, waiting for transfers between devices, take_from(): return lax.ppermute(array, axis, [((i + step) % N, i) for i in range(N)])  56.3 us
    pallas_call x7, Pallas kernels, call(): pl.pallas_call(kernel, grid_spec=pltpu.PrefetchScalarGridSpec(num_scalar_...  45.6 us
    ppermute x15, starting transfers between devices, take_from(): return lax.ppermute(array, axis, [((i + step) % N, i) for i in range(N)])  28 us
    slice x2, local copies, waits for them, and re-layouts, body(): own = [down_weight[:first], down_weight[first:]]  4.49 us
    ppermute x1, waiting for transfers between devices, sum_over_dp(): array = array + lax.ppermute(array, 'y', [(0, 1), (1, 0), (2, 3), (3, 2)])  4.17 us
  transfers between devices with their start and end apart: 22, of which 9 were waited for; matrix products, arithmetic and copies ran while one was open for 4% of the time, Pallas kernels for 26%

profile of v4, /device:TPU:0, one launch (start us, length us, event | category | flops | bytes accessed | tf_op | source)
XLA Modules:
  0.0 179.4 jit_solution(12089848904067830001)
XLA Ops:
  8.1 2.3 %slice.30.refs_0_ = bf16[928,512]{1,0:T(8,128)(2,1)} slice(bf16[1848,512]{1,0:T(8,128)(2,1)} %param.9), slice={[0:928], [0:512]} | slice | bytes 1900544 | tf_op jit(solution)/shard_map/slice | solution.py:340
  17.2 3.3 %shard_map.94 = bf16[128,512]{1,0:T(8,128)(2,1)S(1)} custom-call(s32[4]{0:T(128)S(1)} %gather_fusion, bf16[512,1024]{1,0:T(8,128)(2,1)S(1)} %copy-done.1, bf16[1848,512]{1,0:T(8,128)(2,1)} %bitcast.24, bf16[16,64,1024]{2,1,0:T(8,128)(2,1)} %a_out.1, bf16[16,64,1848]{2,1,0:T(8,128)(2,1)} %a_in.3), custom_call_target="tpu_custom_call" | custom-call | flops 1000000 | bytes 1000000 | tf_op jit(solution)/shard_map/pallas_call | solution.py:49
  20.5 3.5 %collective-permute-start.4 = (bf16[128,512]{1,0:T(8,128)(2,1)S(1)}, bf16[128,512]{1,0:T(8,128)(2,1)S(1)}, u32[]{:S(2)}, u32[]{:S(2)}) collective-permute-start(bf16[128,512]{1,0:T(8,128)(2,1)S(1)} %shard_map.94), channel_id=1, source_target_pairs={{0,16},{16,0},{1,17},{17,1},{2,18},{18,2},{3,19},{19,3},{4,20},{20... | collective-permute-start | bytes 393224 | tf_op jit(solution)/shard_map/ppermute | solution.py:24
  26.7 4.2 %collective-permute-done.5 = bf16[128,512]{1,0:T(8,128)(2,1)S(1)} collective-permute-done((bf16[128,512]{1,0:T(8,128)(2,1)S(1)}, bf16[128,512]{1,0:T(8,128)(2,1)S(1)}, u32[]{:S(2)}, u32[]{:S(2)}) %collective-permute-start.5) | collective-permute-done | bytes 131104 | tf_op jit(solution)/shard_map/ppermute | solution.py:29
  30.9 3.1 %collective-permute-start.6 = (bf16[128,512]{1,0:T(8,128)(2,1)S(1)}, bf16[128,512]{1,0:T(8,128)(2,1)S(1)}, u32[]{:S(2)}, u32[]{:S(2)}) collective-permute-start(bf16[128,512]{1,0:T(8,128)(2,1)S(1)} %add.49), channel_id=1, source_target_pairs={{0,96},{96,0},{32,64},{64,32},{1,97},{97,1},{33,65},{65,33},{2,98}... | collective-permute-start | bytes 393224 | tf_op jit(solution)/shard_map/ppermute | solution.py:30
  38.6 6.5 %shard_map.96 = bf16[4,4,64,2944]{3,2,1,0:T(8,128)(2,1)} custom-call(s32[5]{0:T(128)S(1)} %pad_add_fusion.index, bf16[128,512]{1,0:T(8,128)(2,1)S(1)} %add.50.summed, bf16[512,1024]{1,0:T(8,128)(2,1)S(1)} %copy-done.1, bf16[1848,512]{1,0:T(8,128)(2,1)} %bitcast.25), custom_call_target="tpu_custom_call" | custom-call | flops 1000000 | bytes 1000000 | tf_op jit(solution)/shard_map/pallas_call | solution.py:49
  46.6 3.0 %collective-permute-start.7 = (bf16[920,512]{1,0:T(8,128)(2,1)S(1)}, bf16[920,512]{1,0:T(8,128)(2,1)S(1)}, u32[]{:S(2)}, u32[]{:S(2)}) collective-permute-start(bf16[920,512]{1,0:T(8,128)(2,1)S(1)} %copy-done.6), channel_id=1, source_target_pairs={{4,0},{8,4},{12,8},{0,12},{5,1},{9,5},{13,9},{1,13},{6,2},{10,6},{... | collective-permute-start | bytes 2826248 | tf_op jit(solution)/shard_map/ppermute | solution.py:20
  49.6 19.6 %collective-permute-done.8.refs_3_ = bf16[920,512]{1,0:T(8,128)(2,1)S(1)} collective-permute-done((bf16[920,512]{1,0:T(8,128)(2,1)S(1)}, bf16[920,512]{1,0:T(8,128)(2,1)S(1)}, u32[]{:S(2)}, u32[]{:S(2)}) %collective-permute-start.8) | collective-permute-done | bytes 942112 | tf_op jit(solution)/shard_map/ppermute | solution.py:20
  69.2 3.0 %collective-permute-start.9 = (bf16[928,512]{1,0:T(8,128)(2,1)}, bf16[928,512]{1,0:T(8,128)(2,1)S(1)}, u32[]{:S(2)}, u32[]{:S(2)}) collective-permute-start(bf16[928,512]{1,0:T(8,128)(2,1)} %collective-permute-done.2.refs_1_), channel_id=1, source_target_pairs={{4,0},{8,4},{12,8},{0,12},{5,1},{9,5},{13,9},{1,13},{6,2},{10,6},{... | collective-permute-start | bytes 2850824 | tf_op jit(solution)/shard_map/ppermute | solution.py:20
  72.2 18.4 %collective-permute-done.9.refs_2_ = bf16[928,512]{1,0:T(8,128)(2,1)S(1)} collective-permute-done((bf16[928,512]{1,0:T(8,128)(2,1)}, bf16[928,512]{1,0:T(8,128)(2,1)S(1)}, u32[]{:S(2)}, u32[]{:S(2)}) %collective-permute-start.9) | collective-permute-done | bytes 950304 | tf_op jit(solution)/shard_map/ppermute | solution.py:20
  91.6 8.1 %shard_map.98 = (bf16[928,512]{1,0:T(8,128)(2,1)S(1)}, bf16[928,512]{1,0:T(8,128)(2,1)}) custom-call(s32[3]{0:T(128)S(1)} %get-tuple-element.58.index, bf16[4,2,2,512,512]{4,3,2,1,0:T(8,128)(2,1)} %bitcast.19, bf16[928,512]{1,0:T(8,128)(2,1)} %slice.30.refs_0_, bf16[928,512]{1,0:T(8,128)(2,1)} %collective-permute-done.2.refs_1_, bf16[928,512]{1,0:T(8,128)(2,1)} %copy-done.7, ...), custom_call_target="tpu_custom_call" | custom-call | flops 1000000 | bytes 1000000 | tf_op jit(solution)/shard_map/pallas_call | solution.py:49
  101.0 8.1 %shard_map.101 = (bf16[920,512]{1,0:T(8,128)(2,1)S(1)}, bf16[920,512]{1,0:T(8,128)(2,1)}) custom-call(s32[3]{0:T(128)S(1)} %get-tuple-element.60.index, bf16[4,2,2,512,512]{4,3,2,1,0:T(8,128)(2,1)} %bitcast.20, bf16[920,512]{1,0:T(8,128)(2,1)} %slice.31.refs_0_, bf16[920,512]{1,0:T(8,128)(2,1)} %copy-done.9, ...), custom_call_target="tpu_custom_call" | custom-call | flops 1000000 | bytes 1000000 | tf_op jit(solution)/shard_map/pallas_call | solution.py:49
  109.1 2.5 %collective-permute-start.14 = (bf16[920,512]{1,0:T(8,128)(2,1)S(1)}, bf16[920,512]{1,0:T(8,128)(2,1)S(1)}, u32[]{:S(2)}, u32[]{:S(2)}) collective-permute-start(bf16[920,512]{1,0:T(8,128)(2,1)S(1)} %get-tuple-element.46), channel_id=1, source_target_pairs={{1,0},{2,1},{3,2},{0,3},{5,4},{6,5},{7,6},{4,7},{9,8},{10,9},{11,1... | collective-permute-start | bytes 2826248 | tf_op jit(solution)/shard_map/ppermute | solution.py:20
  111.6 3.2 %collective-permute-start.10 = (bf16[928,512]{1,0:T(8,128)(2,1)}, bf16[928,512]{1,0:T(8,128)(2,1)}, u32[]{:S(2)}, u32[]{:S(2)}) collective-permute-start(bf16[928,512]{1,0:T(8,128)(2,1)} %get-tuple-element.35), channel_id=1, source_target_pairs={{1,0},{2,1},{3,2},{0,3},{5,4},{6,5},{7,6},{4,7},{9,8},{10,9},{11,1... | collective-permute-start | bytes 2850824 | tf_op jit(solution)/shard_map/ppermute | solution.py:20
  114.8 7.2 %shard_map.99 = (bf16[920,512]{1,0:T(8,128)(2,1)S(1)}, bf16[920,512]{1,0:T(8,128)(2,1)S(1)}) custom-call(s32[3]{0:T(128)S(1)} %get-tuple-element.59.index, bf16[4,2,2,512,512]{4,3,2,1,0:T(8,128)(2,1)} %bitcast.21, bf16[920,512]{1,0:T(8,128)(2,1)} %slice.31.refs_0_, bf16[920,512]{1,0:T(8,128)(2,1)} %copy-done.9, ...), custom_call_target="tpu_custom_call" | custom-call | flops 1000000 | bytes 1000000 | tf_op jit(solution)/shard_map/pallas_call | solution.py:49
  123.0 7.2 %shard_map.97 = (bf16[928,512]{1,0:T(8,128)(2,1)S(1)}, bf16[928,512]{1,0:T(8,128)(2,1)S(1)}) custom-call(s32[3]{0:T(128)S(1)} %get-tuple-element.57.index, bf16[4,2,2,512,512]{4,3,2,1,0:T(8,128)(2,1)} %bitcast.22, bf16[928,512]{1,0:T(8,128)(2,1)} %slice.30.refs_0_, bf16[928,512]{1,0:T(8,128)(2,1)} %collective-permute-done.2.refs_1_, ...), custom_call_target="tpu_custom_call" | custom-call | flops 1000000 | bytes 1000000 | tf_op jit(solution)/shard_map/pallas_call | solution.py:49
  130.2 2.8 %collective-permute-done.14 = bf16[920,512]{1,0:T(8,128)(2,1)S(1)} collective-permute-done((bf16[920,512]{1,0:T(8,128)(2,1)S(1)}, bf16[920,512]{1,0:T(8,128)(2,1)S(1)}, u32[]{:S(2)}, u32[]{:S(2)}) %collective-permute-start.14) | collective-permute-done | bytes 942112 | tf_op jit(solution)/shard_map/ppermute | solution.py:20
  134.2 3.6 %collective-permute-start.15 = (bf16[920,512]{1,0:T(8,128)(2,1)}, bf16[920,512]{1,0:T(8,128)(2,1)S(1)}, u32[]{:S(2)}, u32[]{:S(2)}) collective-permute-start(bf16[920,512]{1,0:T(8,128)(2,1)} %add.54), channel_id=1, source_target_pairs={{1,0},{2,1},{3,2},{0,3},{5,4},{6,5},{7,6},{4,7},{9,8},{10,9},{11,1... | collective-permute-start | bytes 2826248 | tf_op jit(solution)/shard_map/ppermute | solution.py:20
  140.6 3.6 %collective-permute-start.19 = (bf16[64,2944]{1,0:T(8,128)(2,1)S(1)}, bf16[64,2944]{1,0:T(8,128)(2,1)S(1)}, u32[]{:S(2)}, u32[]{:S(2)}) collective-permute-start(bf16[64,2944]{1,0:T(8,128)(2,1)S(1)} %get-tuple-element.51), channel_id=1, source_target_pairs={{4,0},{8,4},{12,8},{0,12},{5,1},{9,5},{13,9},{1,13},{6,2},{10,6},{... | collective-permute-start | bytes 1130504 | tf_op jit(solution)/shard_map/ppermute | solution.py:20
  144.2 8.3 %collective-permute-done.19.after = bf16[64,2944]{1,0:T(8,128)(2,1)S(1)} collective-permute-done((bf16[64,2944]{1,0:T(8,128)(2,1)S(1)}, bf16[64,2944]{1,0:T(8,128)(2,1)S(1)}, u32[]{:S(2)}, u32[]{:S(2)}) %collective-permute-start.19) | collective-permute-done | bytes 376864 | tf_op jit(solution)/shard_map/ppermute | solution.py:20
  152.5 2.4 %collective-permute-start.18 = (bf16[64,2944]{1,0:T(8,128)(2,1)S(1)}, bf16[64,2944]{1,0:T(8,128)(2,1)S(1)}, u32[]{:S(2)}, u32[]{:S(2)}) collective-permute-start(bf16[64,2944]{1,0:T(8,128)(2,1)S(1)} %get-tuple-element.52), channel_id=1, source_target_pairs={{8,0},{12,4},{0,8},{4,12},{9,1},{13,5},{1,9},{5,13},{10,2},{14,6},... | collective-permute-start | bytes 1130504 | tf_op jit(solution)/shard_map/ppermute | solution.py:20
  157.0 5.0 %shard_map.100 = (bf16[928,512]{1,0:T(8,128)(2,1)}, bf16[920,512]{1,0:T(8,128)(2,1)S(1)}) custom-call(s32[4]{0:T(128)S(1)} %gather_fusion, bf16[128,512]{1,0:T(8,128)(2,1)S(1)} %add.50.summed, bf16[16,64,1848]{2,1,0:T(8,128)(2,1)} %a_in.3, bf16[928,512]{1,0:T(8,128)(2,1)} %copy-done.3, bf16[928,512]{1,0:T(8,128)(2,1)} %collective-permute-done.10.refs_1_, ...), custom_call_target="tpu_custom_call" | custom-call | flops 1000000 | bytes 1000000 | tf_op jit(solution)/shard_map/pallas_call | solution.py:49
  162.1 3.6 %collective-permute-done.17.across = bf16[64,2944]{1,0:T(8,128)(2,1)S(1)} collective-permute-done((bf16[64,2944]{1,0:T(8,128)(2,1)S(1)}, bf16[64,2944]{1,0:T(8,128)(2,1)S(1)}, u32[]{:S(2)}, u32[]{:S(2)}) %collective-permute-start.17) | collective-permute-done | bytes 376864 | tf_op jit(solution)/shard_map/ppermute | solution.py:20
  166.5 3.5 %collective-permute-done.15.refs_3_ = bf16[920,512]{1,0:T(8,128)(2,1)S(1)} collective-permute-done((bf16[920,512]{1,0:T(8,128)(2,1)}, bf16[920,512]{1,0:T(8,128)(2,1)S(1)}, u32[]{:S(2)}, u32[]{:S(2)}) %collective-permute-start.15) | collective-permute-done | bytes 942112 | tf_op jit(solution)/shard_map/ppermute | solution.py:20
  (69 shorter events, 27.5 us)
Async XLA Ops:
  8.0 82.6 %all-gather.3.cloned.1.call-start = ((), (), s32[]{:S(2)}) async-start(), calls=%async_computation.2 | async-start | bytes 9437184 | tf_op jit(solution)/shard_map/all_gather | solution.py:348
  10.4 27.1 %collective-permute-start.3 = (bf16[928,512]{1,0:T(8,128)(2,1)}, bf16[928,512]{1,0:T(8,128)(2,1)}, u32[]{:S(2)}, u32[]{:S(2)}) collective-permute-start(bf16[928,512]{1,0:T(8,128)(2,1)} %slice.30.refs_0_), channel_id=1, source_target_pairs={{12,0},{0,4},{4,8},{8,12},{13,1},{1,5},{5,9},{9,13},{14,2},{2,6},{... | collective-permute-start | bytes 2850824 | tf_op jit(solution)/shard_map/ppermute | solution.py:20
  11.9 25.5 %collective-permute-start.2 = (bf16[928,512]{1,0:T(8,128)(2,1)}, bf16[928,512]{1,0:T(8,128)(2,1)}, u32[]{:S(2)}, u32[]{:S(2)}) collective-permute-start(bf16[928,512]{1,0:T(8,128)(2,1)} %slice.30.refs_0_), channel_id=1, source_target_pairs={{4,0},{8,4},{12,8},{0,12},{5,1},{9,5},{13,9},{1,13},{6,2},{10,6},{... | collective-permute-start | bytes 2850824 | tf_op jit(solution)/shard_map/ppermute | solution.py:20
  13.7 23.7 %collective-permute-start.1 = (bf16[512,512]{1,0:T(8,128)(2,1)S(1)}, bf16[512,512]{1,0:T(8,128)(2,1)S(1)}, u32[]{:S(2)}, u32[]{:S(2)}) collective-permute-start(bf16[512,512]{1,0:T(8,128)(2,1)S(1)} %get-tuple-element.55), channel_id=1, source_target_pairs={{0,1},{1,0},{2,17},{3,16},{16,3},{17,2},{18,19},{19,18},{4,5},{5,4... | collective-permute-start | bytes 1572872 | tf_op jit(solution)/shard_map/ppermute | solution.py:338
  15.8 21.6 %collective-permute-start = (bf16[512,512]{1,0:T(8,128)(2,1)S(1)}, bf16[512,512]{1,0:T(8,128)(2,1)S(1)}, u32[]{:S(2)}, u32[]{:S(2)}) collective-permute-start(bf16[512,512]{1,0:T(8,128)(2,1)S(1)} %get-tuple-element.56), channel_id=1, source_target_pairs={{0,0},{1,1},{2,16},{3,17},{16,2},{17,3},{18,18},{19,19},{4,4},{5,5... | collective-permute-start | bytes 1572872 | tf_op jit(solution)/shard_map/ppermute | solution.py:338
  20.5 4.5 %collective-permute-start.4 = (bf16[128,512]{1,0:T(8,128)(2,1)S(1)}, bf16[128,512]{1,0:T(8,128)(2,1)S(1)}, u32[]{:S(2)}, u32[]{:S(2)}) collective-permute-start(bf16[128,512]{1,0:T(8,128)(2,1)S(1)} %shard_map.94), channel_id=1, source_target_pairs={{0,16},{16,0},{1,17},{17,1},{2,18},{18,2},{3,19},{19,3},{4,20},{20... | collective-permute-start | bytes 393224 | tf_op jit(solution)/shard_map/ppermute | solution.py:24
  25.1 5.8 %collective-permute-start.5 = (bf16[128,512]{1,0:T(8,128)(2,1)S(1)}, bf16[128,512]{1,0:T(8,128)(2,1)S(1)}, u32[]{:S(2)}, u32[]{:S(2)}) collective-permute-start(bf16[128,512]{1,0:T(8,128)(2,1)S(1)} %add.48), channel_id=1, source_target_pairs={{0,32},{32,0},{64,96},{96,64},{1,33},{33,1},{65,97},{97,65},{2,34}... | collective-permute-start | bytes 393224 | tf_op jit(solution)/shard_map/ppermute | solution.py:29
  30.9 6.4 %collective-permute-start.6 = (bf16[128,512]{1,0:T(8,128)(2,1)S(1)}, bf16[128,512]{1,0:T(8,128)(2,1)S(1)}, u32[]{:S(2)}, u32[]{:S(2)}) collective-permute-start(bf16[128,512]{1,0:T(8,128)(2,1)S(1)} %add.49), channel_id=1, source_target_pairs={{0,96},{96,0},{32,64},{64,32},{1,97},{97,1},{33,65},{65,33},{2,98}... | collective-permute-start | bytes 393224 | tf_op jit(solution)/shard_map/ppermute | solution.py:30
  38.5 100.5 %reduce-scatter.2.cloned.1.call-start = ((), (), s32[]{:S(2)}) async-start(), calls=%async_computation.1 | async-start | bytes 7536640 | tf_op jit(solution)/shard_map/reduce_scatter | solution.py:354
  46.4 22.8 %collective-permute-start.8 = (bf16[920,512]{1,0:T(8,128)(2,1)S(1)}, bf16[920,512]{1,0:T(8,128)(2,1)S(1)}, u32[]{:S(2)}, u32[]{:S(2)}) collective-permute-start(bf16[920,512]{1,0:T(8,128)(2,1)S(1)} %copy-done.6), channel_id=1, source_target_pairs={{12,0},{0,4},{4,8},{8,12},{13,1},{1,5},{5,9},{9,13},{14,2},{2,6},{... | collective-permute-start | bytes 2826248 | tf_op jit(solution)/shard_map/ppermute | solution.py:20
  46.6 22.5 %collective-permute-start.7 = (bf16[920,512]{1,0:T(8,128)(2,1)S(1)}, bf16[920,512]{1,0:T(8,128)(2,1)S(1)}, u32[]{:S(2)}, u32[]{:S(2)}) collective-permute-start(bf16[920,512]{1,0:T(8,128)(2,1)S(1)} %copy-done.6), channel_id=1, source_target_pairs={{4,0},{8,4},{12,8},{0,12},{5,1},{9,5},{13,9},{1,13},{6,2},{10,6},{... | collective-permute-start | bytes 2826248 | tf_op jit(solution)/shard_map/ppermute | solution.py:20
  69.2 30.6 %copy-start.8 = (bf16[920,512]{1,0:T(8,128)(2,1)}, bf16[920,512]{1,0:T(8,128)(2,1)S(1)}, u32[]{:S(2)}) copy-start(bf16[920,512]{1,0:T(8,128)(2,1)S(1)} %collective-permute-done.8.refs_3_) | copy-start | bytes 2826244
  69.2 30.6 %copy-start.9 = (bf16[920,512]{1,0:T(8,128)(2,1)}, bf16[920,512]{1,0:T(8,128)(2,1)S(1)}, u32[]{:S(2)}) copy-start(bf16[920,512]{1,0:T(8,128)(2,1)S(1)} %collective-permute-done.7.refs_1_) | copy-start | bytes 2826244
  69.2 21.5 %collective-permute-start.9 = (bf16[928,512]{1,0:T(8,128)(2,1)}, bf16[928,512]{1,0:T(8,128)(2,1)S(1)}, u32[]{:S(2)}, u32[]{:S(2)}) collective-permute-start(bf16[928,512]{1,0:T(8,128)(2,1)} %collective-permute-done.2.refs_1_), channel_id=1, source_target_pairs={{4,0},{8,4},{12,8},{0,12},{5,1},{9,5},{13,9},{1,13},{6,2},{10,6},{... | collective-permute-start | bytes 2850824 | tf_op jit(solution)/shard_map/ppermute | solution.py:20
  72.1 28.8 %collective-permute-start.11 = (bf16[920,512]{1,0:T(8,128)(2,1)S(1)}, bf16[920,512]{1,0:T(8,128)(2,1)}, u32[]{:S(2)}, u32[]{:S(2)}) collective-permute-start(bf16[920,512]{1,0:T(8,128)(2,1)S(1)} %collective-permute-done.8.refs_3_), channel_id=1, source_target_pairs={{12,0},{0,4},{4,8},{8,12},{13,1},{1,5},{5,9},{9,13},{14,2},{2,6},{... | collective-permute-start | bytes 2826248 | tf_op jit(solution)/shard_map/ppermute | solution.py:20
  99.8 38.0 %collective-permute-start.12 = (bf16[928,512]{1,0:T(8,128)(2,1)S(1)}, bf16[928,512]{1,0:T(8,128)(2,1)S(1)}, u32[]{:S(2)}, u32[]{:S(2)}) collective-permute-start(bf16[928,512]{1,0:T(8,128)(2,1)S(1)} %get-tuple-element.43), channel_id=1, source_target_pairs={{3,0},{0,1},{1,2},{2,3},{7,4},{4,5},{5,6},{6,7},{11,8},{8,9},{9,10... | collective-permute-start | bytes 2850824 | tf_op jit(solution)/shard_map/ppermute | solution.py:20
  109.1 23.9 %collective-permute-start.14 = (bf16[920,512]{1,0:T(8,128)(2,1)S(1)}, bf16[920,512]{1,0:T(8,128)(2,1)S(1)}, u32[]{:S(2)}, u32[]{:S(2)}) collective-permute-start(bf16[920,512]{1,0:T(8,128)(2,1)S(1)} %get-tuple-element.46), channel_id=1, source_target_pairs={{1,0},{2,1},{3,2},{0,3},{5,4},{6,5},{7,6},{4,7},{9,8},{10,9},{11,1... | collective-permute-start | bytes 2826248 | tf_op jit(solution)/shard_map/ppermute | solution.py:20
  111.6 54.9 %collective-permute-start.16 = (bf16[920,512]{1,0:T(8,128)(2,1)}, bf16[920,512]{1,0:T(8,128)(2,1)S(1)}, u32[]{:S(2)}, u32[]{:S(2)}) collective-permute-start(bf16[920,512]{1,0:T(8,128)(2,1)} %get-tuple-element.47), channel_id=1, source_target_pairs={{3,0},{0,1},{1,2},{2,3},{7,4},{4,5},{5,6},{6,7},{11,8},{8,9},{9,10... | collective-permute-start | bytes 2826248 | tf_op jit(solution)/shard_map/ppermute | solution.py:20
  111.6 43.3 %collective-permute-start.10 = (bf16[928,512]{1,0:T(8,128)(2,1)}, bf16[928,512]{1,0:T(8,128)(2,1)}, u32[]{:S(2)}, u32[]{:S(2)}) collective-permute-start(bf16[928,512]{1,0:T(8,128)(2,1)} %get-tuple-element.35), channel_id=1, source_target_pairs={{1,0},{2,1},{3,2},{0,3},{5,4},{6,5},{7,6},{4,7},{9,8},{10,9},{11,1... | collective-permute-start | bytes 2850824 | tf_op jit(solution)/shard_map/ppermute | solution.py:20
  134.2 35.9 %collective-permute-start.15 = (bf16[920,512]{1,0:T(8,128)(2,1)}, bf16[920,512]{1,0:T(8,128)(2,1)S(1)}, u32[]{:S(2)}, u32[]{:S(2)}) collective-permute-start(bf16[920,512]{1,0:T(8,128)(2,1)} %add.54), channel_id=1, source_target_pairs={{1,0},{2,1},{3,2},{0,3},{5,4},{6,5},{7,6},{4,7},{9,8},{10,9},{11,1... | collective-permute-start | bytes 2826248 | tf_op jit(solution)/shard_map/ppermute | solution.py:20
  139.0 31.0 %collective-permute-start.13 = (bf16[928,512]{1,0:T(8,128)(2,1)}, bf16[928,512]{1,0:T(8,128)(2,1)S(1)}, u32[]{:S(2)}, u32[]{:S(2)}) collective-permute-start(bf16[928,512]{1,0:T(8,128)(2,1)} %add.53), channel_id=1, source_target_pairs={{3,0},{0,1},{1,2},{2,3},{7,4},{4,5},{5,6},{6,7},{11,8},{8,9},{9,10... | collective-permute-start | bytes 2850824 | tf_op jit(solution)/shard_map/ppermute | solution.py:20
  140.6 11.9 %collective-permute-start.19 = (bf16[64,2944]{1,0:T(8,128)(2,1)S(1)}, bf16[64,2944]{1,0:T(8,128)(2,1)S(1)}, u32[]{:S(2)}, u32[]{:S(2)}) collective-permute-start(bf16[64,2944]{1,0:T(8,128)(2,1)S(1)} %get-tuple-element.51), channel_id=1, source_target_pairs={{4,0},{8,4},{12,8},{0,12},{5,1},{9,5},{13,9},{1,13},{6,2},{10,6},{... | collective-permute-start | bytes 1130504 | tf_op jit(solution)/shard_map/ppermute | solution.py:20
  152.5 9.6 %collective-permute-start.18 = (bf16[64,2944]{1,0:T(8,128)(2,1)S(1)}, bf16[64,2944]{1,0:T(8,128)(2,1)S(1)}, u32[]{:S(2)}, u32[]{:S(2)}) collective-permute-start(bf16[64,2944]{1,0:T(8,128)(2,1)S(1)} %get-tuple-element.52), channel_id=1, source_target_pairs={{8,0},{12,4},{0,8},{4,12},{9,1},{13,5},{1,9},{5,13},{10,2},{14,6},... | collective-permute-start | bytes 1130504 | tf_op jit(solution)/shard_map/ppermute | solution.py:20
  154.9 10.7 %collective-permute-start.17 = (bf16[64,2944]{1,0:T(8,128)(2,1)S(1)}, bf16[64,2944]{1,0:T(8,128)(2,1)S(1)}, u32[]{:S(2)}, u32[]{:S(2)}) collective-permute-start(bf16[64,2944]{1,0:T(8,128)(2,1)S(1)} %get-tuple-element.53), channel_id=1, source_target_pairs={{12,0},{0,4},{4,8},{8,12},{13,1},{1,5},{5,9},{9,13},{14,2},{2,6},{... | collective-permute-start | bytes 1130504 | tf_op jit(solution)/shard_map/ppermute | solution.py:20
  (9 other events, 59.3 us)
Sparse Core Ops, SparseCore 0:
  38.6 49.7 all-gather.2
Sparse Core Ops, SparseCore 1:
  45.3 65.7 reduce-scatter.1
